TPU v7x, 32 devices: a whole 2x2x4 slice. The times are simulated.
32 devices in a mesh: dp: 8 (over y, x, core), blk: 4 (over z).
Axes of the slice: x: 2, y: 2, z: 4, core: 2. Of those that a mesh axis runs over, the one named last changes fastest.
Arguments:
- patches: bfloat16 [3, 8, 2048, 768], P(None, 'dp', 'blk'), may hold values from -6 to 6
- keep_index: int32 [3, 8, 1024], P(None, 'dp', 'blk'), may hold values from 0 to 511, as said below
- shard_counts: int32 [3, 8, 4], P(None, 'dp'), may hold values from 192 to 256, as said below
- cotangent: bfloat16 [3, 8, 1024, 768], P(None, 'dp', 'blk'), may hold values from -6 to 6
- norm_gain: bfloat16 [768], P(('dp', 'blk')), may hold values from 0.25 to 1.75
- norm_shift: bfloat16 [768], P(('dp', 'blk')), may hold values from -1.75 to 1.75
- qkv_weight: bfloat16 [768, 2304], P(('dp', 'blk')), may hold values from -0.3125 to 0.3125
- query_bias: bfloat16 [768], P(('dp', 'blk')), may hold values from -1.75 to 1.75
- value_bias: bfloat16 [768], P(('dp', 'blk')), may hold values from -1.75 to 1.75
- out_weight: bfloat16 [768, 768], P(('dp', 'blk')), may hold values from -0.875 to 0.875
- out_bias: bfloat16 [768], P(('dp', 'blk')), may hold values from -1.75 to 1.75
- mlp_gain: bfloat16 [768], P(('dp', 'blk')), may hold values from 0.25 to 1.75
- mlp_shift: bfloat16 [768], P(('dp', 'blk')), may hold values from -1.75 to 1.75
- up_weight: bfloat16 [768, 3072], P(('dp', 'blk')), may hold values from -0.21875 to 0.21875
- up_bias: bfloat16 [3072], P(('dp', 'blk')), may hold values from -1.75 to 1.75
- down_weight: bfloat16 [3072, 768], P(('dp', 'blk')), may hold values from -0.109375 to 0.109375
- down_bias: bfloat16 [768], P(('dp', 'blk')), may hold values from -1.75 to 1.75
Outputs:
- activations: bfloat16 [3, 8, 1024, 768], P(None, 'dp', 'blk')
- patch_grad: float32 [3, 8, 2048, 768], P(None, 'dp', 'blk')
- ngain_grad: float32 [768], P(('dp', 'blk'))
- nshift_grad: float32 [768], P(('dp', 'blk'))
- qkv_grad: float32 [768, 2304], P(('dp', 'blk'))
- qbias_grad: float32 [768], P(('dp', 'blk'))
- vbias_grad: float32 [768], P(('dp', 'blk'))
- outw_grad: float32 [768, 768], P(('dp', 'blk'))
- obias_grad: float32 [768], P(('dp', 'blk'))
- mgain_grad: float32 [768], P(('dp', 'blk'))
- mshift_grad: float32 [768], P(('dp', 'blk'))
- upw_grad: float32 [768, 3072], P(('dp', 'blk'))
- ubias_grad: float32 [3072], P(('dp', 'blk'))
- downw_grad: float32 [3072, 768], P(('dp', 'blk'))
- dbias_grad: float32 [768], P(('dp', 'blk'))
Inputs may be any that keep to these rules, and one draw needn't show every extreme that they name: `keep_index`: within each block of 256 entries (one image on one index of blk): distinct rows of that block's 512 patch rows, in ascending order; the first entry of the first block of every image is 0, the class token. `shard_counts`: every image has a block with exactly 256 live slots.
All inputs are finite; a program needn't handle non-finite values.
Results may differ from a plain program's by a relative error of at most 0.014.
The roundings to bfloat16 on the way count: a program that leaves them out, or rounds other values in their place, can miss the bound.
Values may be sent and summed in bfloat16 or wider, within the bound.
A program may use at most 256 MiB of HBM per device.

v0:
```python
import jax
import jax.numpy as jnp
from jax import lax
from jax.sharding import PartitionSpec as P

HEAD = 64


SCALE = 0.125
EPSILON = 1e-06


def layer_norm(rows, gain, shift):
    center = jnp.mean(rows, axis=-1, keepdims=True)
    centred = rows - center
    spread = jnp.mean(centred * centred, axis=-1, keepdims=True)
    return centred * lax.rsqrt(spread + EPSILON) * gain + shift


def gelu_exact(values):
    return jax.nn.gelu(values, approximate=False)


def inner_rows(left, right):
    return lax.dot_general(
        left, right, (((0,), (0,)), ((), ())), preferred_element_type=jnp.float32
    )


def inner_cols(left, right):
    return lax.dot_general(
        left, right, (((1,), (1,)), ((), ())), preferred_element_type=jnp.float32
    )


def column_sums(values):
    return jnp.sum(values.astype(jnp.float32), axis=0)


def live_masks(counts, capacity, blocks, mine):
    shard_ids = jnp.arange(blocks, dtype=jnp.int32)
    own_count = jnp.sum(jnp.where(shard_ids == mine, counts, 0))
    live_rows = jnp.arange(capacity, dtype=jnp.int32) < own_count
    places = jnp.arange(blocks * capacity, dtype=jnp.int32)
    owner = places // capacity
    limits = jnp.sum(jnp.where(owner[:, None] == shard_ids[None, :], counts[None, :], 0), axis=1)
    live_keys = places % capacity < limits
    return (live_rows, live_keys)


def body(
    patches,
    keep_index,
    shard_counts,
    cotangent,
    norm_gain,
    norm_shift,
    qkv_weight,
    query_bias,
    value_bias,
    out_weight,
    out_bias,
    mlp_gain,
    mlp_shift,
    up_weight,
    up_bias,
    down_weight,
    down_bias,
):
    shards = (
        norm_gain,
        norm_shift,
        qkv_weight,
        query_bias,
        value_bias,
        out_weight,
        out_bias,
        mlp_gain,
        mlp_shift,
        up_weight,
        up_bias,
        down_weight,
        down_bias,
    )
    batches = patches.shape[0]
    patch_count = patches.shape[2]
    width = patches.shape[3]
    capacity = keep_index.shape[2]
    heads = width // HEAD
    blocks = lax.axis_size("blk")
    mine = lax.axis_index("blk")
    totals = None
    outputs = []
    patch_grads = []
    for batch in range(batches):
        front = (
            lax.all_gather(shards[0], ("dp", "blk"), axis=0, tiled=True),
            lax.all_gather(shards[1], ("dp", "blk"), axis=0, tiled=True),
            lax.all_gather(shards[2], ("dp", "blk"), axis=0, tiled=True),
            lax.all_gather(shards[3], ("dp", "blk"), axis=0, tiled=True),
            lax.all_gather(shards[4], ("dp", "blk"), axis=0, tiled=True),
            lax.all_gather(shards[5], ("dp", "blk"), axis=0, tiled=True),
            lax.all_gather(shards[6], ("dp", "blk"), axis=0, tiled=True),
            lax.all_gather(shards[7], ("dp", "blk"), axis=0, tiled=True),
            lax.all_gather(shards[8], ("dp", "blk"), axis=0, tiled=True),
            lax.all_gather(shards[9], ("dp", "blk"), axis=0, tiled=True),
            lax.all_gather(shards[10], ("dp", "blk"), axis=0, tiled=True),
            lax.all_gather(shards[11], ("dp", "blk"), axis=0, tiled=True),
            lax.all_gather(shards[12], ("dp", "blk"), axis=0, tiled=True),
        )
        (
            gain_one,
            shift_one,
            mix_weight,
            bias_query,
            bias_value,
            proj_weight,
            bias_proj,
            gain_two,
            shift_two,
            expand_weight,
            bias_expand,
            shrink_weight,
            bias_shrink,
        ) = front
        live_rows, live_keys = live_masks(shard_counts[batch, 0], capacity, blocks, mine)
        live_float = live_rows.astype(jnp.float32)[:, None]
        keep = keep_index[batch, 0]
        rows = jnp.take(patches[batch, 0], keep, axis=0).astype(jnp.float32)
        normed, norm_back = jax.vjp(
            layer_norm, rows, gain_one.astype(jnp.float32), shift_one.astype(jnp.float32)
        )
        normed_low = normed.astype(jnp.bfloat16)
        mixed = jnp.dot(normed_low, mix_weight, preferred_element_type=jnp.float32)
        query_low = (mixed[:, :width] + bias_query.astype(jnp.float32)).astype(jnp.bfloat16)
        keys_low = mixed[:, width : 2 * width].astype(jnp.bfloat16)
        values_low = (mixed[:, 2 * width :] + bias_value.astype(jnp.float32)).astype(jnp.bfloat16)
        all_keys, all_values = (
            lax.all_gather(keys_low, "blk", axis=0, tiled=True),
            lax.all_gather(values_low, "blk", axis=0, tiled=True),
        )
        query_heads = query_low.reshape(capacity, heads, HEAD)
        key_heads = all_keys.reshape(-1, heads, HEAD)
        value_heads = all_values.reshape(-1, heads, HEAD)
        scores = (
            jnp.einsum("qhd,khd->hqk", query_heads, key_heads, preferred_element_type=jnp.float32)
            * SCALE
        )
        scores = jnp.where(live_keys[None, None, :], scores, -1e30)
        attention = jax.nn.softmax(scores, axis=-1)
        attention_low = attention.astype(jnp.bfloat16)
        attended = jnp.einsum(
            "hqk,khd->qhd", attention_low, value_heads, preferred_element_type=jnp.float32
        )
        attended = attended.reshape(capacity, width).astype(jnp.bfloat16)
        middle = (
            rows
            + jnp.dot(attended, proj_weight, preferred_element_type=jnp.float32)
            + bias_proj.astype(jnp.float32)
        )
        normed_two, norm_back_two = jax.vjp(
            layer_norm, middle, gain_two.astype(jnp.float32), shift_two.astype(jnp.float32)
        )
        normed_two_low = normed_two.astype(jnp.bfloat16)
        hidden = jnp.dot(
            normed_two_low, expand_weight, preferred_element_type=jnp.float32
        ) + bias_expand.astype(jnp.float32)
        active, gelu_back = jax.vjp(gelu_exact, hidden)
        active_low = active.astype(jnp.bfloat16)
        result = jnp.dot(
            active_low, shrink_weight, preferred_element_type=jnp.float32
        ) + bias_shrink.astype(jnp.float32)
        outputs.append((live_float * (middle + result)).astype(jnp.bfloat16))
        back = (
            lax.all_gather(shards[0], ("dp", "blk"), axis=0, tiled=True),
            lax.all_gather(shards[1], ("dp", "blk"), axis=0, tiled=True),
            lax.all_gather(shards[2], ("dp", "blk"), axis=0, tiled=True),
            lax.all_gather(shards[3], ("dp", "blk"), axis=0, tiled=True),
            lax.all_gather(shards[4], ("dp", "blk"), axis=0, tiled=True),
            lax.all_gather(shards[5], ("dp", "blk"), axis=0, tiled=True),
            lax.all_gather(shards[6], ("dp", "blk"), axis=0, tiled=True),
            lax.all_gather(shards[7], ("dp", "blk"), axis=0, tiled=True),
            lax.all_gather(shards[8], ("dp", "blk"), axis=0, tiled=True),
            lax.all_gather(shards[9], ("dp", "blk"), axis=0, tiled=True),
            lax.all_gather(shards[10], ("dp", "blk"), axis=0, tiled=True),
            lax.all_gather(shards[11], ("dp", "blk"), axis=0, tiled=True),
            lax.all_gather(shards[12], ("dp", "blk"), axis=0, tiled=True),
        )
        mix_back, proj_back, expand_back, shrink_back = (back[2], back[5], back[9], back[11])
        outer = live_float * cotangent[batch, 0].astype(jnp.float32)
        outer_low = outer.astype(jnp.bfloat16)
        grad_shrink = inner_rows(active_low, outer_low)
        grad_shrink_bias = column_sums(outer_low)
        grad_active = inner_cols(outer_low, shrink_back)
        grad_hidden_low = gelu_back(grad_active)[0].astype(jnp.bfloat16)
        grad_expand = inner_rows(normed_two_low, grad_hidden_low)
        grad_expand_bias = column_sums(grad_hidden_low)
        grad_normed_two = inner_cols(grad_hidden_low, expand_back)
        grad_middle_part, grad_gain_two, grad_shift_two = norm_back_two(grad_normed_two)
        grad_middle = outer + grad_middle_part
        branch_low = grad_middle.astype(jnp.bfloat16)
        grad_proj = inner_rows(attended, branch_low)
        grad_proj_bias = column_sums(branch_low)
        grad_attended = inner_cols(branch_low, proj_back).astype(jnp.bfloat16)
        attended_heads = grad_attended.reshape(capacity, heads, HEAD)
        grad_attention = jnp.einsum(
            "qhd,khd->hqk", attended_heads, value_heads, preferred_element_type=jnp.float32
        )
        weighted = jnp.sum(attention * grad_attention, axis=-1, keepdims=True)
        grad_scores_low = (attention * (grad_attention - weighted)).astype(jnp.bfloat16)
        grad_query = (
            jnp.einsum(
                "hqk,khd->qhd", grad_scores_low, key_heads, preferred_element_type=jnp.float32
            )
            * SCALE
        )
        row_total = jax.nn.logsumexp(scores, axis=-1)
        every_query, every_grad = (
            lax.all_gather(query_low, "blk", axis=0, tiled=True),
            lax.all_gather(grad_attended, "blk", axis=0, tiled=True),
        )
        every_total, every_weighted = (
            lax.all_gather(row_total, "blk", axis=1, tiled=True),
            lax.all_gather(weighted[:, :, 0], "blk", axis=1, tiled=True),
        )
        every_query_heads = every_query.reshape(-1, heads, HEAD)
        every_grad_heads = every_grad.reshape(-1, heads, HEAD)
        own_keys = keys_low.reshape(capacity, heads, HEAD)
        own_values = values_low.reshape(capacity, heads, HEAD)
        own_scores = (
            jnp.einsum(
                "qhd,khd->hqk", every_query_heads, own_keys, preferred_element_type=jnp.float32
            )
            * SCALE
        )
        own_scores = jnp.where(live_rows[None, None, :], own_scores, -1e30)
        own_probs = jnp.exp(own_scores - every_total[:, :, None])
        own_grad_probs = jnp.einsum(
            "qhd,khd->hqk", every_grad_heads, own_values, preferred_element_type=jnp.float32
        )
        own_grad_scores = (own_probs * (own_grad_probs - every_weighted[:, :, None])).astype(
            jnp.bfloat16
        )
        grad_keys = (
            jnp.einsum(
                "hqk,qhd->khd",
                own_grad_scores,
                every_query_heads,
                preferred_element_type=jnp.float32,
            )
            * SCALE
        )
        grad_values = jnp.einsum(
            "hqk,qhd->khd",
            own_probs.astype(jnp.bfloat16),
            every_grad_heads,
            preferred_element_type=jnp.float32,
        )
        grad_keys = grad_keys.reshape(capacity, width)
        grad_values = grad_values.reshape(capacity, width)
        grad_mixed_low = jnp.concatenate(
            [grad_query.reshape(capacity, width), grad_keys, grad_values], axis=1
        ).astype(jnp.bfloat16)
        grad_mix = inner_rows(normed_low, grad_mixed_low)
        grad_query_bias = column_sums(grad_mixed_low[:, :width])
        grad_value_bias = column_sums(grad_mixed_low[:, 2 * width :])
        grad_normed = inner_cols(grad_mixed_low, mix_back)
        grad_rows_part, grad_gain_one, grad_shift_one = norm_back(grad_normed)
        grad_rows = grad_middle + grad_rows_part
        patch_grads.append(jnp.zeros((patch_count, width), jnp.float32).at[keep].add(grad_rows))
        local = (
            grad_gain_one,
            grad_shift_one,
            grad_mix,
            grad_query_bias,
            grad_value_bias,
            grad_proj,
            grad_proj_bias,
            grad_gain_two,
            grad_shift_two,
            grad_expand,
            grad_expand_bias,
            grad_shrink,
            grad_shrink_bias,
        )
        totals = local if totals is None else jax.tree.map(jnp.add, totals, local)
    totals = lax.psum_scatter(totals, ("dp", "blk"), scatter_dimension=0, tiled=True)
    activations = jnp.stack(outputs)[:, None]
    patch_grad = jnp.stack(patch_grads)[:, None]
    return (
        activations,
        patch_grad,
        totals[0],
        totals[1],
        totals[2],
        totals[3],
        totals[4],
        totals[5],
        totals[6],
        totals[7],
        totals[8],
        totals[9],
        totals[10],
        totals[11],
        totals[12],
    )


def solution(mesh):
    in_specs = (
        P(None, "dp", "blk", None),
        P(None, "dp", "blk"),
        P(None, "dp", None),
        P(None, "dp", "blk", None),
        P(("dp", "blk")),
        P(("dp", "blk")),
        P(("dp", "blk"), None),
        P(("dp", "blk")),
        P(("dp", "blk")),
        P(("dp", "blk"), None),
        P(("dp", "blk")),
        P(("dp", "blk")),
        P(("dp", "blk")),
        P(("dp", "blk"), None),
        P(("dp", "blk")),
        P(("dp", "blk"), None),
        P(("dp", "blk")),
    )
    out_specs = (
        P(None, "dp", "blk", None),
        P(None, "dp", "blk", None),
        P(("dp", "blk")),
        P(("dp", "blk")),
        P(("dp", "blk"), None),
        P(("dp", "blk")),
        P(("dp", "blk")),
        P(("dp", "blk"), None),
        P(("dp", "blk")),
        P(("dp", "blk")),
        P(("dp", "blk")),
        P(("dp", "blk"), None),
        P(("dp", "blk")),
        P(("dp", "blk"), None),
        P(("dp", "blk")),
    )
    return jax.shard_map(body, mesh=mesh, in_specs=in_specs, out_specs=out_specs, check_vma=False)
```

profile of v0, /device:TPU:5, one launch (start us, length us, event | category | flops | bytes accessed | tf_op | source)
XLA Modules:
  0.0 1234.7 jit_solution(5317937225375213099)
XLA Ops:
  15.5 40.9 %all-reduce.19 = (bf16[768]{0:T(1024)(128)(2,1)S(1)}, bf16[768]{0:T(1024)(128)(2,1)S(1)}, bf16[768]{0:T(1024)(128)(2,1)S(1)}, bf16[768]{0:T(1024)(128)(2,1)S(1)}...) all-reduce(bf16[768]{0:T(1024)(128)(2,1)S(1)} %dynamic-update-slice, ...), channel_id=1, replica_groups=mesh['dp'=8,'blk'=4] {'dp','blk'}, use_global_device_ids=true, to_apply=%add.1 | all-reduce | flops 9216 | bytes 36864
  63.4 9.3 all-gather.17.cloned.1.call-done
  132.4 19.4 %all-gather.33.cloned.1.call-done = bf16[1024,768]{1,0:T(8,128)(2,1)} async-done(((bf16[256,768]{1,0:T(8,128)(2,1)}), bf16[1024,768]{1,0:T(8,128)(2,1)}) %all-gather.33.cloned.1.call-update) | async-done | bytes 1572880 | tf_op jit(solution)/shard_map/all_gather | solution.py:140
  154.4 6.8 fusion.87
  161.3 46.7 %all-gather.23.cloned.1.call-done = bf16[768,768]{1,0:T(8,128)(2,1)} async-done(((bf16[24,768]{1,0:T(8,128)(2,1)}), bf16[768,768]{1,0:T(8,128)(2,1)}) %all-gather.23.cloned.1.call-update) | async-done | bytes 1179664 | tf_op jit(solution)/shard_map/all_gather | solution.py:102
  210.8 34.1 %all-gather.21.cloned.1.call-done = bf16[1024,768]{1,0:T(8,128)(2,1)} async-done(((bf16[256,768]{1,0:T(8,128)(2,1)}), bf16[1024,768]{1,0:T(8,128)(2,1)}) %all-gather.21.cloned.1.call-update) | async-done | bytes 1572880 | tf_op jit(solution)/shard_map/all_gather | solution.py:139
  256.4 26.0 %all-gather.19.cloned.1.call-done = bf16[1024,768]{1,0:T(8,128)(2,1)} async-done(((bf16[256,768]{1,0:T(8,128)(2,1)}), bf16[1024,768]{1,0:T(8,128)(2,1)}) %all-gather.19.cloned.1.call-update) | async-done | bytes 1572880 | tf_op jit(solution)/shard_map/all_gather | solution.py:140
  285.0 6.9 fusion.81
  293.4 26.6 %all-gather.31.cloned.1.call-done = bf16[1024,768]{1,0:T(8,128)(2,1)} async-done(((bf16[256,768]{1,0:T(8,128)(2,1)}), bf16[1024,768]{1,0:T(8,128)(2,1)}) %all-gather.31.cloned.1.call-update) | async-done | bytes 1572880 | tf_op jit(solution)/shard_map/all_gather | solution.py:139
  333.7 23.8 %all-gather.29.cloned.1.call-done = bf16[1024,768]{1,0:T(8,128)(2,1)} async-done(((bf16[256,768]{1,0:T(8,128)(2,1)}), bf16[1024,768]{1,0:T(8,128)(2,1)}) %all-gather.29.cloned.1.call-update) | async-done | bytes 1572880 | tf_op jit(solution)/shard_map/all_gather | solution.py:140
  360.1 6.8 fusion.84
  370.2 53.2 %all-gather.25.cloned.1.call-done = bf16[768,3072]{1,0:T(8,128)(2,1)} async-done(((bf16[24,3072]{1,0:T(8,128)(2,1)}), bf16[768,3072]{1,0:T(8,128)(2,1)}) %all-gather.25.cloned.1.call-update) | async-done | bytes 4718608 | tf_op jit(solution)/shard_map/all_gather | solution.py:106
  423.3 11.8 multiply_convert_fusion.12
  435.2 11.1 multiply_convert_fusion.13
  446.3 11.6 multiply_convert_fusion.14
  457.9 30.4 %all-gather.27.cloned.1.call-done = bf16[3072,768]{1,0:T(8,128)(2,1)} async-done(((bf16[96,768]{1,0:T(8,128)(2,1)}), bf16[3072,768]{1,0:T(8,128)(2,1)}) %all-gather.27.cloned.1.call-update) | async-done | bytes 4718608 | tf_op jit(solution)/shard_map/all_gather | solution.py:108
  488.4 7.0 convert_reduce_fusion
  520.3 13.2 %multiply_reduce_fusion.1 = (f32[12,256]{1,0:T(8,128)S(1)}, f32[12,256]{1,0:T(8,128)S(1)}, f32[12,256,1024]{2,1,0:T(8,128)}) fusion(f32[12,256]{1,0:T(8,128)S(1)} %copy-done.128, f32[12,256]{1,0:T(8,128)S(1)} %copy-done.105, f32[12,256,1024]{2,1,0:T(8,128)} %copy-done.2, pred[1024]{0:T(1024)(128)(4,1)S(1)} %copy-done.191, ...), kind=kOutput, calls=%fused_computation.15 | convolution fusion | flops 427812864 | bytes 27194368 | tf_op jit(solution)/shard_map/qhd,khd->hqk/dot_general | solution.py:206
  533.5 11.5 all_gather.155
  545.0 11.5 all_gather.157
  559.1 11.6 fusion.94
  570.8 13.2 %multiply_reduce_fusion.2 = (f32[12,256]{1,0:T(8,128)S(1)}, f32[12,256]{1,0:T(8,128)S(1)}, f32[12,256,1024]{2,1,0:T(8,128)}) fusion(f32[12,256]{1,0:T(8,128)S(1)} %copy-done.126, f32[12,256]{1,0:T(8,128)S(1)} %copy-done.103, f32[12,256,1024]{2,1,0:T(8,128)} %copy-done.1, pred[1024]{0:T(1024)(128)(4,1)S(1)} %copy-done.189, ...), kind=kOutput, calls=%fused_computation.20 | convolution fusion | flops 427812864 | bytes 27194368 | tf_op jit(solution)/shard_map/qhd,khd->hqk/dot_general | solution.py:206
  584.0 11.9 all_gather.151
  595.9 11.2 all_gather.153
  607.9 12.1 fusion.93
  620.1 12.2 multiply_reduce_fusion
  632.3 11.6 all_gather.159
  643.9 11.4 all_gather.161
  657.0 6.4 fusion.281
  665.2 6.4 fusion.279
  673.4 7.9 fusion.283
  683.2 12.1 fusion.95
  698.4 7.4 fusion.99
  705.7 10.6 fusion.79
  719.0 6.7 fusion.96
  725.8 10.2 fusion.78
  736.0 4.9 fusion.168
  742.9 5.0 fusion.166
  748.0 6.8 fusion.102
  754.9 9.2 fusion.80
  764.1 9.3 add_add_fusion.2
  779.4 6.9 add_add_fusion.1
  792.2 5.1 add_add_fusion
  826.4 55.3 %all-reduce.18 = (f32[768]{0:T(1024)S(1)}, f32[768]{0:T(1024)S(1)}, f32[768]{0:T(1024)S(1)}, f32[768]{0:T(1024)S(1)}, f32[768]{0:T(1024)S(1)}, /*index=5*/f32[76...) all-reduce(f32[768]{0:T(1024)S(1)} %add_add_fusion.18, ...), channel_id=2, replica_groups=mesh['dp'=8,'blk'=4] {'dp','blk'}, use_global_device_ids=true, to_apply=%region_48.50.clone | all-reduce | flops 9216 | bytes 73728
  901.2 4.9 maximum_bitcast_fusion
  906.1 38.6 %reduce-scatter.5.cloned.1.call-done = f32[24,2304]{1,0:T(8,128)} async-done(((f32[768,2304]{1,0:T(8,128)}), f32[24,2304]{1,0:T(8,128)}) %reduce-scatter.5.cloned.1.call-update) | async-done | bytes 221200 | tf_op jit(solution)/shard_map/reduce_scatter | solution.py:287
  944.7 141.0 %reduce-scatter.9.cloned.1.call-done = f32[24,3072]{1,0:T(8,128)} async-done(((f32[768,3072]{1,0:T(8,128)}), f32[24,3072]{1,0:T(8,128)}) %reduce-scatter.9.cloned.1.call-update) | async-done | bytes 294928 | tf_op jit(solution)/shard_map/reduce_scatter | solution.py:287
  1085.7 142.0 %reduce-scatter.11.cloned.1.call-done = f32[96,768]{1,0:T(8,128)} async-done(((f32[3072,768]{1,0:T(8,128)}), f32[96,768]{1,0:T(8,128)}) %reduce-scatter.11.cloned.1.call-update) | async-done | bytes 294928 | tf_op jit(solution)/shard_map/reduce_scatter | solution.py:287
  (715 shorter events, 216.6 us)
Async XLA Ops:
  7.2 65.5 %all-gather.17.cloned.1.call-start = ((), (), s32[]{:S(2)}) async-start(), calls=%async_computation.4 | async-start | bytes 3649536 | tf_op jit(solution)/shard_map/all_gather | solution.py:99
  7.9 110.9 %all-gather.35.cloned.1.call-start = ((), (), s32[]{:S(2)}) async-start(), calls=%async_computation.13 | async-start | bytes 1966080 | tf_op jit(solution)/shard_map/all_gather | solution.py:139
  60.1 147.9 %copy-start.3 = (bf16[256,768]{1,0:T(8,128)(2,1)}, bf16[256,768]{1,0:T(8,128)(2,1)S(1)}, u32[]{:S(2)}) copy-start(bf16[256,768]{1,0:T(8,128)(2,1)S(1)} %gather_fusion.2) | copy-start | bytes 1179652
  61.4 230.6 %copy-start.8 = (bf16[256,768]{1,0:T(8,128)(2,1)}, bf16[256,768]{1,0:T(8,128)(2,1)S(1)}, u32[]{:S(2)}) copy-start(bf16[256,768]{1,0:T(8,128)(2,1)S(1)} %gather_fusion) | copy-start | bytes 1179652
  62.6 304.3 %copy-start.10 = (bf16[256,768]{1,0:T(8,128)(2,1)}, bf16[256,768]{1,0:T(8,128)(2,1)S(1)}, u32[]{:S(2)}) copy-start(bf16[256,768]{1,0:T(8,128)(2,1)S(1)} %gather_fusion.1) | copy-start | bytes 1179652
  62.6 145.4 %copy-start.167 = (pred[256]{0:T(512)(128)(4,1)}, pred[256]{0:T(512)(128)(4,1)S(1)}, u32[]{:S(2)}) copy-start(pred[256]{0:T(512)(128)(4,1)S(1)} %compare_and_fusion) | copy-start | bytes 772
  62.9 229.1 %copy-start.170 = (pred[256]{0:T(512)(128)(4,1)}, pred[256]{0:T(512)(128)(4,1)S(1)}, u32[]{:S(2)}) copy-start(pred[256]{0:T(512)(128)(4,1)S(1)} %compare_and_fusion.2) | copy-start | bytes 772
  78.2 73.6 %all-gather.33.cloned.1.call-start = ((), (), s32[]{:S(2)}) async-start(), calls=%async_computation.12 | async-start | bytes 1966080 | tf_op jit(solution)/shard_map/all_gather | solution.py:140
  87.3 120.7 %all-gather.23.cloned.1.call-start = ((), (), s32[]{:S(2)}) async-start(), calls=%async_computation.7 | async-start | bytes 1216512 | tf_op jit(solution)/shard_map/all_gather | solution.py:102
  87.9 157.1 %all-gather.21.cloned.1.call-start = ((), (), s32[]{:S(2)}) async-start(), calls=%async_computation.6 | async-start | bytes 1966080 | tf_op jit(solution)/shard_map/all_gather | solution.py:139
  89.9 192.4 %all-gather.19.cloned.1.call-start = ((), (), s32[]{:S(2)}) async-start(), calls=%async_computation.5 | async-start | bytes 1966080 | tf_op jit(solution)/shard_map/all_gather | solution.py:140
  90.5 229.5 %all-gather.31.cloned.1.call-start = ((), (), s32[]{:S(2)}) async-start(), calls=%async_computation.11 | async-start | bytes 1966080 | tf_op jit(solution)/shard_map/all_gather | solution.py:139
  92.5 265.0 %all-gather.29.cloned.1.call-start = ((), (), s32[]{:S(2)}) async-start(), calls=%async_computation.10 | async-start | bytes 1966080 | tf_op jit(solution)/shard_map/all_gather | solution.py:140
  93.3 330.0 %all-gather.25.cloned.1.call-start = ((), (), s32[]{:S(2)}) async-start(), calls=%async_computation.8 | async-start | bytes 4866048 | tf_op jit(solution)/shard_map/all_gather | solution.py:106
  94.0 394.4 %all-gather.27.cloned.1.call-start = ((), (), s32[]{:S(2)}) async-start(), calls=%async_computation.9 | async-start | bytes 4866048 | tf_op jit(solution)/shard_map/all_gather | solution.py:108
  94.6 560.7 %all-gather.41.cloned.1.call-start = ((), (), s32[]{:S(2)}) async-start(), calls=%async_computation.16 | async-start | bytes 1966080 | tf_op jit(solution)/shard_map/all_gather | solution.py:219
  95.3 568.1 %all-gather.37.cloned.1.call-start = ((), (), s32[]{:S(2)}) async-start(), calls=%async_computation.14 | async-start | bytes 1966080 | tf_op jit(solution)/shard_map/all_gather | solution.py:219
  95.9 575.7 %all-gather.45.cloned.1.call-start = ((), (), s32[]{:S(2)}) async-start(), calls=%async_computation.18 | async-start | bytes 1966080 | tf_op jit(solution)/shard_map/all_gather | solution.py:219
  98.5 347.8 %copy-start.84 = (f32[768]{0:T(1024)}, f32[768]{0:T(1024)S(1)}, u32[]{:S(2)}) copy-start(f32[768]{0:T(1024)S(1)} %convert_element_type.312) | copy-start | bytes 9220
  99.2 412.6 %copy-start.80 = (f32[768]{0:T(1024)}, f32[768]{0:T(1024)S(1)}, u32[]{:S(2)}) copy-start(f32[768]{0:T(1024)S(1)} %convert_element_type.311) | copy-start | bytes 9220
  118.3 577.5 %all-gather.43.cloned.1.call-start = ((), (), s32[]{:S(2)}) async-start(), calls=%async_computation.17 | async-start | bytes 1966080 | tf_op jit(solution)/shard_map/all_gather | solution.py:220
  154.4 53.6 %copy-start.211 = (f32[768]{0:T(1024)S(1)}, f32[768]{0:T(1024)}, u32[]{:S(2)}) copy-start(f32[768]{0:T(1024)} %convert_element_type.310) | copy-start | bytes 9220
  161.3 49.6 %copy-start.95 = (bf16[12,64,256]{2,1,0:T(8,128)(2,1)}, bf16[12,64,256]{2,1,0:T(8,128)(2,1)S(1)}, u32[]{:S(2)}) copy-start(bf16[12,64,256]{2,1,0:T(8,128)(2,1)S(1)} %fusion.87) | copy-start | bytes 1179652
  208.0 38.7 %copy-start.75 = (bf16[256,768]{0,1:T(8,128)(2,1)S(1)}, bf16[256,768]{0,1:T(8,128)(2,1)}, u32[]{:S(2)}) copy-start(bf16[256,768]{0,1:T(8,128)(2,1)} %copy.114) | copy-start | bytes 1179652
  209.9 213.4 %copy-start.18 = (f32[256,768]{1,0:T(8,128)}, f32[256,768]{1,0:T(8,128)S(1)}, u32[]{:S(2)}) copy-start(f32[256,768]{1,0:T(8,128)S(1)} %get-tuple-element.195) | copy-start | bytes 2359300
  209.9 36.7 %copy-start.188 = (pred[1024]{0:T(1024)(128)(4,1)S(1)}, pred[1024]{0:T(1024)(128)(4,1)}, u32[]{:S(2)}) copy-start(pred[1024]{0:T(1024)(128)(4,1)} %fusion.196) | copy-start | bytes 3076
  293.4 218.4 %copy-start.111 = (f32[256]{0:T(256)}, f32[256]{0:T(256)S(1)}, u32[]{:S(2)}) copy-start(f32[256]{0:T(256)S(1)} %broadcast_multiply_fusion.4) | copy-start | bytes 3076
  366.9 68.2 %copy-start.92 = (bf16[12,64,256]{2,1,0:T(8,128)(2,1)}, bf16[12,64,256]{2,1,0:T(8,128)(2,1)S(1)}, u32[]{:S(2)}) copy-start(bf16[12,64,256]{2,1,0:T(8,128)(2,1)S(1)} %fusion.84) | copy-start | bytes 1179652
  367.6 144.3 %copy-start.113 = (f32[256]{0:T(256)}, f32[256]{0:T(256)S(1)}, u32[]{:S(2)}) copy-start(f32[256]{0:T(256)S(1)} %broadcast_multiply_fusion.2) | copy-start | bytes 3076
  370.1 65.0 %copy-start.154 = (f32[256]{0:T(256)}, f32[256]{0:T(256)S(1)}, u32[]{:S(2)}) copy-start(f32[256]{0:T(256)S(1)} %get-tuple-element.222) | copy-start | bytes 3076
  370.2 65.0 %copy-start.177 = (f32[3072]{0:T(1024)S(1)}, f32[3072]{0:T(1024)}, u32[]{:S(2)}) copy-start(f32[3072]{0:T(1024)} %convert_element_type.314) | copy-start | bytes 36868
  446.3 42.0 %copy-start.5 = (bf16[3,1,256,768]{3,2,1,0:T(8,128)(2,1)S(1)}, bf16[3,1,256,768]{3,2,1,0:T(8,128)(2,1)}, u32[]{:S(2)}) copy-start(bf16[3,1,256,768]{3,2,1,0:T(8,128)(2,1)} %param.22) | copy-start | bytes 3538948
  446.3 42.0 %copy-start.183 = (f32[256]{0:T(256)S(1)}, f32[256]{0:T(256)}, u32[]{:S(2)}) copy-start(f32[256]{0:T(256)} %fusion.225) | copy-start | bytes 3076
  514.2 92.9 %copy-start.44 = (bf16[256,768]{1,0:T(8,128)(2,1)}, bf16[256,768]{1,0:T(8,128)(2,1)S(1)}, u32[]{:S(2)}) copy-start(bf16[256,768]{1,0:T(8,128)(2,1)S(1)} %get-tuple-element.162) | copy-start | bytes 1179652
  520.2 196.2 %all-gather.39.cloned.1.call-start = ((), (), s32[]{:S(2)}) async-start(), calls=%async_computation.15 | async-start | bytes 1966080 | tf_op jit(solution)/shard_map/all_gather | solution.py:220
  520.3 36.2 %copy-start.91 = (bf16[12,64,256]{2,1,0:T(8,128)(2,1)S(1)}, bf16[12,64,256]{2,1,0:T(8,128)(2,1)}, u32[]{:S(2)}) copy-start(bf16[12,64,256]{2,1,0:T(8,128)(2,1)} %copy-done.90) | copy-start | bytes 1179652
  570.7 170.3 %all-gather.47.cloned.1.call-start = ((), (), s32[]{:S(2)}) async-start(), calls=%async_computation.19 | async-start | bytes 1966080 | tf_op jit(solution)/shard_map/all_gather | solution.py:220
  620.0 286.1 %reduce-scatter.7.cloned.1.call-start = ((), (), s32[]{:S(2)}) async-start(), calls=%async_computation.21 | async-start | bytes 2433024 | tf_op jit(solution)/shard_map/reduce_scatter | solution.py:287
  695.3 249.4 %reduce-scatter.5.cloned.1.call-start = ((), (), s32[]{:S(2)}) async-start(), calls=%async_computation.20 | async-start | bytes 7299072 | tf_op jit(solution)/shard_map/reduce_scatter | solution.py:287
  773.5 312.2 %reduce-scatter.9.cloned.1.call-start = ((), (), s32[]{:S(2)}) async-start(), calls=%async_computation.22 | async-start | bytes 9732096 | tf_op jit(solution)/shard_map/reduce_scatter | solution.py:287
  786.4 441.3 %reduce-scatter.11.cloned.1.call-start = ((), (), s32[]{:S(2)}) async-start(), calls=%async_computation.23 | async-start | bytes 9732096 | tf_op jit(solution)/shard_map/reduce_scatter | solution.py:287
  824.9 66.3 %copy-start.226 = (f32[256]{0:T(256)S(1)}, f32[256]{0:T(256)}, u32[]{:S(2)}) copy-start(f32[256]{0:T(256)} %get-tuple-element.167) | copy-start | bytes 3076
  824.9 66.3 %copy-start.122 = (f32[256]{0:T(256)S(1)}, f32[256]{0:T(256)}, u32[]{:S(2)}) copy-start(f32[256]{0:T(256)} %copy-done.119) | copy-start | bytes 3076
  825.0 66.3 %copy-start.150 = (f32[256]{0:T(256)S(1)}, f32[256]{0:T(256)}, u32[]{:S(2)}) copy-start(f32[256]{0:T(256)} %get-tuple-element.220) | copy-start | bytes 3076
  825.0 66.3 %copy-start.166 = (f32[256]{0:T(256)S(1)}, f32[256]{0:T(256)}, u32[]{:S(2)}) copy-start(f32[256]{0:T(256)} %copy-done.163) | copy-start | bytes 3076
  825.0 66.3 %copy-start.176 = (pred[256]{0:T(512)(128)(4,1)S(1)}, pred[256]{0:T(512)(128)(4,1)}, u32[]{:S(2)}) copy-start(pred[256]{0:T(512)(128)(4,1)} %copy-done.173) | copy-start | bytes 772
  825.0 66.3 %copy-start.209 = (f32[256]{0:T(256)S(1)}, f32[256]{0:T(256)}, u32[]{:S(2)}) copy-start(f32[256]{0:T(256)} %copy-done.208) | copy-start | bytes 3076
  825.0 66.3 %copy-start.224 = (f32[256]{0:T(256)S(1)}, f32[256]{0:T(256)}, u32[]{:S(2)}) copy-start(f32[256]{0:T(256)} %copy-done.223) | copy-start | bytes 3076
  (213 other events, 1515.4 us)
Sparse Core Ops, SparseCore 0:
  10.8 61.8 all-gather.16
  78.3 35.3 all-gather.34
  115.8 35.9 all-gather.32
  154.5 53.4 all-gather.22
  209.4 35.4 all-gather.20
  246.4 35.9 all-gather.18
  283.9 36.0 all-gather.30
  321.6 35.8 all-gather.28
  360.3 62.9 all-gather.24
  426.0 62.3 all-gather.26
  489.9 35.3 all-gather.40
  526.7 38.0 all-gather.36
  566.4 37.2 all-gather.44
  605.2 36.5 all-gather.42
  643.2 36.6 all-gather.38
  681.3 35.8 all-gather.46
  722.9 96.3 reduce-scatter.6
  826.4 118.2 reduce-scatter.4
  951.1 134.5 reduce-scatter.8
  1093.0 134.5 reduce-scatter.10
where the time goes:
time: 1250 us; the launch traced here: 1230 us
  waiting for transfers between devices  596 us (48%)
  matrix products  309 us (25%)
  blocking collectives  165 us (13%)
  local copies, waits for them, and re-layouts  84.9 us (7%)
  other arithmetic  59.8 us (5%)
  between operations  17.7 us (1%)
    reduce_scatter x4, waiting for transfers between devices, body(): lax.psum_scatter(totals, ('dp', 'blk'), scatter_dimension=0, tiled=True)  322 us
    unnamed x2, blocking collectives  96.2 us
    all_gather x3, waiting for transfers between devices, body(): lax.all_gather(values_low, 'blk', axis=0, tiled=True)  69.1 us
    all_gather x3, waiting for transfers between devices, body(): lax.all_gather(keys_low, 'blk', axis=0, tiled=True)  60.8 us
    all_gather x1, waiting for transfers between devices, body(): lax.all_gather(shards[9], ('dp', 'blk'), axis=0, tiled=True)  53.2 us
    dot_general x12, matrix products, inner_rows(): lax.dot_general(left, right, (((0,), (0,)), ((), ())), preferred_element_...  47.2 us
    all_gather x1, waiting for transfers between devices, body(): lax.all_gather(shards[5], ('dp', 'blk'), axis=0, tiled=True)  46.7 us
    dot_general x3, matrix products, body(): jnp.einsum('qhd,khd->hqk', attended_heads, value_heads, preferred_element...  38.5 us
  transfers between devices with their start and end apart: 20, of which 12 were waited for; matrix products, arithmetic and copies ran while one was open for 34% of the time, Pallas kernels for 0%

commit v1 on v0

v1 whole, which is shorter than its diff:
```python
import functools

import jax
import jax.numpy as jnp
from jax import lax
from jax.experimental import pallas as pl
from jax.experimental.pallas import tpu as pltpu
from jax.sharding import PartitionSpec as P

MESH = pl.DeviceIdType.MESH
ANY = pl.BlockSpec(memory_space=pl.ANY)
VMEM = pl.BlockSpec(memory_space=pltpu.VMEM)
SMEM = pl.BlockSpec(memory_space=pltpu.SMEM)
f32, bf16, i32 = jnp.float32, jnp.bfloat16, jnp.int32

EPSILON = 1e-06
LOG2E = 1.4426950408889634
NEG = -1e30


def nn(a, b):
    return lax.dot_general(a, b, (((1,), (0,)), ((), ())), preferred_element_type=f32)


def nt(a, b):
    return lax.dot_general(a, b, (((1,), (1,)), ((), ())), preferred_element_type=f32)


def tn(a, b):
    return lax.dot_general(a, b, (((0,), (0,)), ((), ())), preferred_element_type=f32)


def mult(x, k):
    return x if isinstance(x, int) else pl.multiple_of(x, k)


def normalise(v):
    centred = v - jnp.mean(v, axis=1, keepdims=True)
    inv = lax.rsqrt(jnp.mean(centred * centred, axis=1, keepdims=True) + EPSILON)
    return centred * inv, inv


def norm_back(e, n, inv, gain):
    f = e * gain
    return inv * (f - jnp.mean(f, axis=1, keepdims=True) - n * jnp.mean(f * n, axis=1, keepdims=True))


def col_sum(v):
    return jnp.sum(v, axis=0, keepdims=True)


V_NG, V_NS, V_QB, V_VB, V_OB, V_MG, V_MS, V_DB, V_UB = range(9)


def layer_kernel(cfg, names_in, names_out, names_scratch, *refs):
    R = dict(zip(names_in + names_out + names_scratch, refs, strict=True))
    aligned, dps = cfg["aligned"], cfg["dps"]
    T, W, F = cfg["tokens"], cfg["width"], cfg["ff"]
    KR = W // dps
    FR = F // dps
    HALF = W // 2
    dp, z = lax.axis_index("dp"), lax.axis_index("blk")
    c = lax.rem(dp, 2)
    base = dp - c
    h, e = lax.div(z, 2), lax.rem(z, 2)
    g = 2 * e + c
    other = base + 1 - c
    ss, rs = R["ss"], R["rs"]
    count = [0]

    def take(n=1):
        count[0] += n
        return count[0] - n

    def rcopy(src, dst, s, r, dev):
        return pltpu.make_async_remote_copy(
            src_ref=src, dst_ref=dst, send_sem=ss.at[s], recv_sem=rs.at[r], device_id=dev, device_id_type=MESH
        )

    def recv(dst, r, dev=None):
        rcopy(dst, dst, 0, r, (other, z) if dev is None else dev).wait_recv()

    bar = pltpu.get_barrier_semaphore()
    peers = []
    for k in range(1, 8):
        j = lax.rem(c * 4 + z + k, 8)
        peers.append((base + lax.div(j, 4), lax.rem(j, 4)))
    if aligned:
        dx = 2 - 4 * lax.rem(lax.div(dp, 2), 2)
        dy = 4 - 8 * lax.div(dp, 4)
        p1, p2, p3 = dp + (1 - c) * dx + c * dy, dp + c * dx + (1 - c) * dy, dp + dx + dy
        peers += [(p1, z), (p2, z)]
    for dev in peers:
        pl.semaphore_signal(bar, inc=1, device_id=dev, device_id_type=MESH)

    def owner(m):
        if m < 2:
            return lax.div(z, 2), 2 * c + m, lax.rem(z, 2)
        return lax.rem(z, 2), 2 * c + lax.div(z, 2), 2

    def home(s):
        if s < 2:
            return h, 2 * c + s
        return h, 2 * e + c

    def move_out(m, src, dst, sid, rid):
        tc, tz, slot = owner(m)
        own = jnp.logical_and(tc == c, tz == z)

        @pl.when(own)
        def _():
            pltpu.make_async_copy(src, dst.at[slot], rs.at[rid + slot]).start()

        @pl.when(jnp.logical_not(own))
        def _():
            rcopy(src, dst.at[slot], sid + m, rid + slot, (base + tc, tz)).start()

    def move_out_done(m, src, dst, sid, rid):
        tc, tz, slot = owner(m)
        own = jnp.logical_and(tc == c, tz == z)

        @pl.when(jnp.logical_not(own))
        def _():
            rcopy(src, dst.at[slot], sid + m, rid + slot, (base + tc, tz)).wait_send()

    def move_home(s, src, dst, sid, rid):
        tc, tz = home(s)
        m = e if s < 2 else 2
        own = jnp.logical_and(tc == c, tz == z)

        @pl.when(own)
        def _():
            pltpu.make_async_copy(src, dst.at[m], ss.at[sid + s]).start()

        @pl.when(jnp.logical_not(own))
        def _():
            rcopy(src, dst.at[m], sid + s, rid + m, (base + tc, tz)).start()

    def move_home_done(s, src, dst, sid, rid):
        tc, tz = home(s)
        m = e if s < 2 else 2
        own = jnp.logical_and(tc == c, tz == z)

        @pl.when(own)
        def _():
            pltpu.make_async_copy(src, dst.at[m], ss.at[sid + s]).wait()

        @pl.when(jnp.logical_not(own))
        def _():
            rcopy(src, dst.at[m], sid + s, rid + m, (base + tc, tz)).wait_send()

    def arrived_home(m, dst, rid):
        tc, tz, _ = owner(m)

        @pl.when(jnp.logical_not(jnp.logical_and(tc == c, tz == z)))
        def _():
            recv(dst.at[m], rid + m)

    arrays = [R["wq"], R["wo"], R["wu"], R["wd"]]
    Q_, O_, U_, D_ = 0, 1, 2, 3
    if aligned:
        zbuf, zrr, zrl = R["zbuf"], R["zrr"], R["zrl"]
        flat = cfg["flat"]
        CH = {"Q": (0, flat[1]), "O": (flat[1], flat[2]), "U": (flat[2], flat[3]), "D": (flat[3], flat[4]), "V": (flat[4], flat[5])}
        ZR = {k: take(3) - 1 for k in CH}
        ZL = {k: take(3) - 1 for k in CH}
        YR = {k: take(3) - 1 for k in "QOUD"}
        YL = {k: take(3) - 1 for k in "QOUD"}
        gathered = arrays + [R["vw"]]
        XY = [take(3) for _ in range(5)]
        CR = [take(4) for _ in range(5)]
        R1 = [take(4) for _ in range(4)]
        R2 = [take(3) for _ in range(4)]

        def z_send(key, k, done=False):
            r0, r1 = CH[key]
            rows = pl.ds(r0, r1 - r0)
            right = jnp.logical_and(z < 3, z - (k - 1) >= 0)
            left = jnp.logical_and(z > 0, z + (k - 1) <= 3)

            @pl.when(right)
            def _():
                ref = zbuf.at[z - (k - 1), rows]
                d = rcopy(ref, ref, ZR[key] + k, ZR[key] + k, (dp, z + 1))
                d.wait_send() if done else d.start()

            @pl.when(left)
            def _():
                ref = zbuf.at[z + (k - 1), rows]
                d = rcopy(ref, ref, ZL[key] + k, ZL[key] + k, (dp, z - 1))
                d.wait_send() if done else d.start()

        def z_wait(key, k):
            r0, r1 = CH[key]
            rows = pl.ds(r0, r1 - r0)

            @pl.when(z - k >= 0)
            def _():
                recv(zbuf.at[z - k, rows], ZR[key] + k)

            @pl.when(z + k <= 3)
            def _():
                recv(zbuf.at[z + k, rows], ZL[key] + k)

        def flatten(a, ref, slot, block=None):
            if a == D_:
                n, rows = W // 128, FR // 4
            elif a == 4:
                n, rows = 1, 16
            else:
                n, rows = ref.shape[-1] // 128, KR // 4
            for t in range(n):
                cols = slice(t * 128, (t + 1) * 128)
                piece = ref[:, cols] if block is None else ref[block, slot * rows : (slot + 1) * rows, cols]
                zbuf[slot, flat[a] + t * rows : flat[a] + (t + 1) * rows, :] = piece

        def unflatten(a, block):
            dst = gathered[a]
            if a == D_:
                n, rows = W // 128, FR // 4
            elif a == 4:
                n, rows = 1, 16
            else:
                n, rows = dst.shape[-1] // 128, KR // 4
            for s in range(4):
                for t in range(n):
                    dst[block, s * rows : (s + 1) * rows, t * 128 : (t + 1) * 128] = zbuf[s, flat[a] + t * rows : flat[a] + (t + 1) * rows, :]

        def ag_copies(a):
            ref = gathered[a]

            def core(i):
                block = (dp, p1, p2, p3)[i]
                return rcopy(ref.at[block], ref.at[block], CR[a] + i, CR[a] + i, (other, z))

            return {
                "p1": lambda: rcopy(ref.at[dp], ref.at[dp], XY[a], XY[a], (p1, z)),
                "p2": lambda: rcopy(ref.at[dp], ref.at[dp], XY[a] + 1, XY[a] + 1, (p2, z)),
                "fw": lambda: rcopy(ref.at[p1], ref.at[p1], XY[a] + 2, XY[a] + 2, (p2, z)),
                "c0": lambda: core(0),
                "c1": lambda: core(1),
                "c2": lambda: core(2),
                "c3": lambda: core(3),
            }

        def ag1(a):
            d = ag_copies(a)
            d["p1"]().start()
            d["p2"]().start()
            d["c0"]().start()

        def ag2(a):
            d = ag_copies(a)
            ref = gathered[a]
            recv(ref.at[p1], XY[a])
            d["fw"]().start()
            d["c1"]().start()
            recv(ref.at[p2], XY[a] + 1)
            d["c2"]().start()

        def ag3(a):
            d = ag_copies(a)
            recv(gathered[a].at[p3], XY[a] + 2)
            d["c3"]().start()

        def ag4(a):
            d = ag_copies(a)
            for i, block in enumerate((dp, p2, p1, p3)):
                recv(gathered[a].at[block + other - dp], CR[a] + i)
            for k in d.values():
                k().wait_send()

        def blk_of(i):
            return 2 * i + c

        bufs1 = [R["rb1" + n] for n in "qoud"]
        bufs2 = [R["rb2" + n] for n in "qoud"]

        def view(buf, a, i):
            r, w = arrays[a].shape[1:]
            return buf.at[i, pl.ds(0, r), pl.ds(0, w)]

        def rs_core(a, i):
            return rcopy(arrays[a].at[2 * i + 1 - c], view(bufs1[a], a, i), R1[a] + i, R1[a] + i, (other, z))

        def rs1(a):
            for i in range(4):
                rs_core(a, i).start()

        def addto(ref, block, parts):
            rows, width = ref.shape[1:]
            step = 96

            @pl.loop(0, rows // step)
            def _(q):
                r = pl.ds(mult(q * step, step), step)
                total = ref[block, r, :].astype(f32)
                for p, i in parts:
                    total = total + p[i, r, pl.ds(0, width)].astype(f32)
                ref[block, r, :] = total.astype(bf16)

        def rs_xy(a):
            ref = arrays[a]
            return {
                "diag": lambda: rcopy(ref.at[p3], view(bufs2[a], a, 0), R2[a], R2[a], (p2, z)),
                "p2": lambda: rcopy(ref.at[p2], view(bufs2[a], a, 1), R2[a] + 1, R2[a] + 1, (p2, z)),
                "p1": lambda: rcopy(ref.at[p1], view(bufs2[a], a, 2), R2[a] + 2, R2[a] + 2, (p1, z)),
            }

        def rs2(a):
            for i in range(4):
                recv(view(bufs1[a], a, i), R1[a] + i)
                addto(arrays[a], blk_of(i), [(bufs1[a], i)])
            d = rs_xy(a)
            d["diag"]().start()
            d["p2"]().start()

        def rs3(a):
            recv(view(bufs2[a], a, 0), R2[a])
            addto(arrays[a], p1, [(bufs2[a], 0)])
            rs_xy(a)["p1"]().start()

        def rs4(a):
            recv(view(bufs2[a], a, 1), R2[a] + 1)
            recv(view(bufs2[a], a, 2), R2[a] + 2)
            addto(arrays[a], dp, [(bufs2[a], 1), (bufs2[a], 2)])
            for s in range(4):
                flatten(a, arrays[a], s, dp)
            y_send("QOUD"[a], 1)

        def y_send(key, k, done=False):
            r0, r1 = CH[key]
            rows = pl.ds(r0, r1 - r0)
            to_right = z + 4 - k
            to_left = z - 4 + k

            @pl.when(jnp.logical_and(z < 3, to_right <= 3))
            def _():
                if k > 1 and not done:

                    @pl.when(z >= 1)
                    def _():
                        recv(zrr.at[k - 2, rows], YR[key] + k - 1)
                        zbuf[to_right, rows, :] = (zbuf[to_right, rows, :].astype(f32) + zrr[k - 2, rows, :].astype(f32)).astype(bf16)

                d = rcopy(zbuf.at[to_right, rows], zrr.at[k - 1, rows], YR[key] + k, YR[key] + k, (dp, z + 1))
                d.wait_send() if done else d.start()

            @pl.when(jnp.logical_and(z > 0, to_left >= 0))
            def _():
                if k > 1 and not done:

                    @pl.when(z <= 2)
                    def _():
                        recv(zrl.at[k - 2, rows], YL[key] + k - 1)
                        zbuf[to_left, rows, :] = (zbuf[to_left, rows, :].astype(f32) + zrl[k - 2, rows, :].astype(f32)).astype(bf16)

                d = rcopy(zbuf.at[to_left, rows], zrl.at[k - 1, rows], YL[key] + k, YL[key] + k, (dp, z - 1))
                d.wait_send() if done else d.start()

        def y_final(a, out):
            key = "QOUD"[a]
            r0, r1 = CH[key]
            rows = pl.ds(r0, r1 - r0)

            @pl.when(z >= 1)
            def _():
                recv(zrr.at[2, rows], YR[key] + 3)

            @pl.when(z <= 2)
            def _():
                recv(zrl.at[2, rows], YL[key] + 3)

            if a == D_:
                n, step = W // 128, FR // 4
            else:
                n, step = out.shape[-1] // 128, KR // 4
            for t in range(n):
                piece = slice(r0 + t * step, r0 + (t + 1) * step)
                total = zbuf[z, piece, :].astype(f32)
                total = total + jnp.where(z >= 1, zrr[2, piece, :].astype(f32), 0.0)
                total = total + jnp.where(z <= 2, zrl[2, piece, :].astype(f32), 0.0)
                out[:, t * 128 : (t + 1) * 128] = total
            for k in (1, 2, 3):
                y_send(key, k, done=True)
            for i in range(4):
                rs_core(a, i).wait_send()
            for d in rs_xy(a).values():
                d().wait_send()

        outs = [R["gq"], R["go"], R["gu"], R["gd"]]

    I_ROWS, I_CNT, I_COT, I_ACT, I_GR = (take(3) for _ in range(5))
    S_ROWS, S_CNT, S_COT, S_ACT, S_GR = (take(3) for _ in range(5))
    EX = {}
    for k in ("qkv", "att", "do", "dqkv"):
        EX[k] = (take(1), take(4), take(4))
    L0 = take(12)

    rows, cot, cnt, nbuf = R["rows"], R["cot"], R["cnt"], R["nbuf"]
    qkv, qkva, qkvb = R["qkv"], R["qkva"], R["qkvb"]
    atta, attb, att, fromb = R["atta"], R["attb"], R["att"], R["fromb"]
    doa, dob, mid, vt, vg = R["doa"], R["dob"], R["mid"], R["vt"], R["vg"]
    lse, grh, keep, act = R["lse"], R["grh"], R["keep"], R["act"]
    lane = lax.broadcasted_iota(i32, (1, 128), 1)

    if aligned:
        for a, name in enumerate(("sq", "so", "su", "sd", "sv")):
            flatten(a, R[name], z)
    for m in range(3):
        for b in range(4):
            R["cnth"][m, b : b + 1, :] = jnp.full((1, 128), R["counts"][m, b], i32).astype(f32).astype(bf16)
        R["cnth"][m, 4:, :] = jnp.zeros((12, 128), bf16)

    pl.semaphore_wait(bar, len(peers))
    if aligned:
        z_send("Q", 1)
        z_send("V", 1)

    def pick_rows(pbuf, psem):
        copies = [pltpu.make_async_copy(R["patches"].at[m], pbuf.at[m], psem.at[m]) for m in range(3)]
        for d in copies:
            d.start()
        for m in range(3):
            copies[m].wait()
            spread = (lax.broadcasted_iota(i32, (cfg["patch"], T), 0) == keep[m]).astype(f32).astype(bf16)
            att[0, m * T : (m + 1) * T, :] = tn(spread, pbuf[m]).astype(bf16)
            move_out(m, att.at[0, pl.ds(m * T, T)], rows, S_ROWS, I_ROWS)
            move_out(m, R["cnth"].at[m], cnt, S_CNT, I_CNT)

    pl.run_scoped(pick_rows, pltpu.VMEM((3, cfg["patch"], W), bf16), pltpu.SemaphoreType.DMA((3,)))
    if aligned:
        for k in (1, 2):
            for key in "QV":
                z_wait(key, k)
                z_send(key, k + 1)
        for key in "OUD":
            z_send(key, 1)
        for key in "QV":
            z_wait(key, 3)
        unflatten(Q_, dp)
        ag1(Q_)
        unflatten(4, dp)
        ag1(4)
    else:
        full = [pltpu.make_async_copy(R[n], arrays[i], rs.at[L0 + 8 + i]) for i, n in enumerate(("sq", "so", "su", "sd"))]
        for d in full:
            d.start()
    for m in range(3):
        move_out(m, R["cotangent"].at[m], cot, S_COT, I_COT)
    if aligned:
        ag2(Q_)
        ag2(4)
        for key in "OUD":
            z_wait(key, 1)
            z_send(key, 2)
        ag3(Q_)
        ag3(4)
        ag4(4)
        v = R["vw"][...].reshape(32 * 16, 128)
        to = lax.broadcasted_iota(i32, (128, W), 1)
        frm = lax.broadcasted_iota(i32, (128, W), 0)
        dev = lax.broadcasted_iota(i32, (512, W), 0) // 16
        col = lax.broadcasted_iota(i32, (512, W), 1)
        n1, n2 = W // 32, F // 32
        x1 = nn(v, (lax.rem(to, n1) == frm).astype(f32).astype(bf16))
        x1 = jnp.where(dev == col // n1, x1, 0.0)
        vt[0:16, :] = jnp.sum(x1.reshape(32, 16, W), axis=0)
        x2 = nn(v, (lax.rem(to, n2) == frm).astype(f32).astype(bf16))
        x2 = jnp.where(lax.rem(dev, W // n2) == col // n2, x2, 0.0)
        x2 = jnp.sum(x2.reshape(4, 8, 16, W), axis=1)
        for q in range(4):
            vt[V_UB + q : V_UB + q + 1, :] = x2[q, V_UB : V_UB + 1, :]
    else:
        vt[...] = R["sv"][...]

    def vec(i):
        return vt[i : i + 1, :]

    def normed_rows(s):
        n, _ = normalise(rows[s].astype(f32))
        nbuf[s] = (n * vec(V_NG) + vec(V_NS)).astype(bf16)

    for s in range(3):
        recv(rows.at[s], I_ROWS + s)
        recv(cnt.at[s], I_CNT + s)
        normed_rows(s)
    if aligned:
        ag4(Q_)
        for key in "OUD":
            z_wait(key, 2)
            z_send(key, 3)
    else:
        for d in full:
            d.wait()

    def wblock(ref, cols=None):
        v = ref[...] if cols is None else ref[:, :, cols]
        return v.reshape(-1, v.shape[-1])

    def project(s):
        for j in range(3):
            v = nn(nbuf[s], wblock(R["wq"], slice(j * W, (j + 1) * W)))
            if j == 0:
                v = v + vec(V_QB)
            if j == 2:
                v = v + vec(V_VB)
            qkv[j, pl.ds(mult(s * T, T), T), :] = v.astype(bf16)

    def dev_of(i):
        return (base + lax.rem(i, 2), 2 * h + lax.div(i, 2))

    def ds128(x, n):
        return pl.ds(mult(x, 128), n)

    def to_heads_a(kind, src, dst):
        i0 = EX[kind][0]
        full_ = [slice(None)] * (len(src.shape) - 2)
        sref = src.at[(*full_, pl.ds(0, 2 * T), ds128(HALF * (1 - c), HALF))]
        dref = dst.at[(*full_, ds128(2 * T * c, 2 * T))]
        return rcopy(sref, dref, i0, i0, (other, z))

    def to_heads_a_own(kind, src, dst, lid):
        full_ = [slice(None)] * (len(src.shape) - 2)
        sref = src.at[(*full_, pl.ds(0, 2 * T), ds128(HALF * c, HALF))]
        dref = dst.at[(*full_, ds128(2 * T * c, 2 * T))]
        return pltpu.make_async_copy(sref, dref, rs.at[lid])

    def to_heads_b(kind, src, dst, k):
        _, rid, sid = EX[kind]
        full_ = [slice(None)] * (len(src.shape) - 2)
        t = lax.rem(g + k, 4)
        sref = src.at[(*full_, pl.ds(2 * T, T), ds128(HALF * lax.div(t, 2) + 128 * lax.rem(t, 2), 256))]
        dref = dst.at[(*full_, ds128(T * g, T))]
        return rcopy(sref, dref, sid + k, rid + k, dev_of(t))

    def to_heads_b_own(kind, src, dst, lid):
        full_ = [slice(None)] * (len(src.shape) - 2)
        sref = src.at[(*full_, pl.ds(2 * T, T), ds128(HALF * e + 128 * c, 256))]
        dref = dst.at[(*full_, ds128(T * g, T))]
        return pltpu.make_async_copy(sref, dref, rs.at[lid])

    def from_heads_a(kind, src, dst):
        i0 = EX[kind][0]
        full_ = [slice(None)] * (len(src.shape) - 2)
        sref = src.at[(*full_, ds128(2 * T * (1 - c), 2 * T))]
        dref = dst.at[(*full_, pl.ds(0, 2 * T), ds128(HALF * c, HALF))]
        return rcopy(sref, dref, i0, i0, (other, z))

    def from_heads_a_own(kind, src, dst, lid):
        full_ = [slice(None)] * (len(src.shape) - 2)
        sref = src.at[(*full_, ds128(2 * T * c, 2 * T))]
        dref = dst.at[(*full_, pl.ds(0, 2 * T), ds128(HALF * c, HALF))]
        return pltpu.make_async_copy(sref, dref, rs.at[lid])

    def from_heads_b(kind, src, j0, k):
        _, rid, sid = EX[kind]
        t = lax.rem(g + k, 4)
        n = src.shape[0]
        sref = src.at[:, ds128(T * t, T)]
        dref = fromb.at[g, pl.ds(0, n)]
        return rcopy(sref, dref, sid + k, rid + k, dev_of(t))

    def from_heads_b_own(src, lid):
        n = src.shape[0]
        return pltpu.make_async_copy(src.at[:, ds128(T * g, T)], fromb.at[g, pl.ds(0, n)], rs.at[lid])

    def wait_a(kind, dst, heads):
        full_ = [slice(None)] * (len(dst.shape) - 2)
        if heads:
            dref = dst.at[(*full_, ds128(2 * T * (1 - c), 2 * T))]
        else:
            dref = dst.at[(*full_, pl.ds(0, 2 * T), ds128(HALF * (1 - c), HALF))]
        recv(dref, EX[kind][0])

    def wait_b_heads(kind, dst):
        full_ = [slice(None)] * (len(dst.shape) - 2)
        for k in (1, 2, 3):
            recv(dst.at[(*full_, ds128(T * lax.rem(g + 4 - k, 4), T))], EX[kind][1] + k)

    def wait_b_tokens(kind, n):
        for k in (1, 2, 3):
            recv(fromb.at[lax.rem(g + 4 - k, 4), pl.ds(0, n)], EX[kind][1] + k)

    def merge_b(dst, j, n_from):
        for q in range(2):
            lo, hi = fromb[2 * q, n_from], fromb[2 * q + 1, n_from]
            at = q * HALF
            dst[j, 2 * T : 3 * T, at : at + 128] = lo[:, 0:128]
            dst[j, 2 * T : 3 * T, at + 128 : at + 256] = jnp.where(lane < 64, lo[:, 128:256], hi[:, 0:128])
            dst[j, 2 * T : 3 * T, at + 256 : at + 384] = hi[:, 128:256]

    @pl.loop(0, 2)
    def _(s):
        project(s)

    for m in range(3):
        move_out_done(m, att.at[0, pl.ds(m * T, T)], rows, S_ROWS, I_ROWS)
    xa = to_heads_a("qkv", qkv, qkva)
    xa.start()
    la = to_heads_a_own("qkv", qkv, qkva, L0)
    la.start()
    project(2)
    xb = [to_heads_b("qkv", qkv, qkvb, k) for k in (1, 2, 3)]
    for d in xb:
        d.start()
    lb = to_heads_b_own("qkv", qkv, qkvb, L0 + 1)
    lb.start()

    def weights_ready(step):
        if not aligned:
            return
        if step == 0:
            for key in "OUD":
                z_wait(key, 3)
            for a in (O_, U_, D_):
                unflatten(a, dp)
                ag1(a)
        elif step == 1:
            for a in (O_, U_, D_):
                ag2(a)
        elif step == 2:
            for a in (O_, U_, D_):
                ag3(a)
        elif step == 3:
            for a in (O_, U_, D_):
                ag4(a)
            for key in CH:
                for k in (1, 2, 3):
                    z_send(key, k, done=True)

    def key_bias(slot):
        parts = []
        at = lax.broadcasted_iota(i32, (T, 128), 0).astype(f32)
        for b in range(4):
            limit = cnt[slot, b : b + 1, :].astype(f32)
            parts.append(jnp.where(at < limit, 0.0, NEG))
        return jnp.concatenate(parts, axis=0).astype(bf16)

    bias = R["bias"]
    bias[0] = key_bias(0)
    bias[1] = key_bias(2)
    QT = 256
    N = 4 * T

    def half(i, x):
        return jnp.where(lane // 64 == i, x, jnp.zeros_like(x))

    def key_side(k2, b, i):
        spot = 64 * (1 - i)
        return jnp.where(lane // 64 == i, k2, jnp.where(lane == spot, b, jnp.zeros_like(b)))

    def query_side(q2, i):
        spot = 64 * (1 - i)
        return jnp.where(lane // 64 == i, q2, jnp.where(lane == spot, 1.0, 0.0).astype(bf16))

    SC = 0.125 * LOG2E

    def attend(src, dst, col, bi, sel, lrow):
        cols = ds128(col, 128)
        k2 = src[1, :, cols]
        b = bias[bi]
        keys = [key_side(k2, b, i) for i in sel]

        @pl.loop(0, N // QT)
        def _(q):
            r = ds128(q * QT, QT)
            q2 = src[0, r, cols]
            v2 = src[2, :, cols]
            outs = []
            for n, i in enumerate(sel):
                s = nt(query_side(q2, i), keys[n])
                top = jnp.max(s, axis=1, keepdims=True) * SC
                p = jnp.exp2(s * SC - top)
                total = jnp.sum(p, axis=1, keepdims=True)
                outs.append(nn(p.astype(bf16), v2) / total)
                full_total = jnp.broadcast_to(top + jnp.log2(total), (QT, 128)).T
                lse[pl.ds(lrow + n, 1), r] = full_total[0:1, :]
            if len(sel) == 2:
                o = jnp.where(lane < 64, outs[0], outs[1])
            else:
                o = jnp.where(lane // 64 == sel[0], outs[0], 0.0)
            dst[0, r, cols] = o.astype(bf16)

    la.wait()
    wait_a("qkv", qkva, True)

    @pl.loop(0, 2)
    def _(t):
        attend(qkva, atta, t * 128, 0, (0, 1), 2 * t)

    weights_ready(0)
    attend(qkva, atta, 256, 0, (0, 1), 4)
    xatt = from_heads_a("att", atta, att)
    xatt.start()
    latt = from_heads_a_own("att", atta, att, L0 + 2)
    latt.start()
    lb.wait()
    wait_b_heads("qkv", qkvb)
    weights_ready(1)
    attend(qkvb, attb, c * 128, 1, (0, 1), 6)
    weights_ready(2)
    attend(qkvb, attb, (1 - c) * 128, 1, (c,), 8)
    xattb = [from_heads_b("att", attb, 0, k) for k in (1, 2, 3)]
    for d in xattb:
        d.start()
    lattb = from_heads_b_own(attb, L0 + 3)
    lattb.start()
    weights_ready(3)
    xa.wait_send()
    for d in xb:
        d.wait_send()
    latt.wait()
    wait_a("att", att, False)
    lattb.wait()
    wait_b_tokens("att", 1)
    merge_b(att, 0, 0)

    def slot_rows(s):
        return pl.ds(mult(s * T, T), T)

    for s in range(3):
        recv(cot.at[s], I_COT + s)

    def live_of(s):
        b = 2 * c + s if s < 2 else g
        at = lax.broadcasted_iota(i32, (T, 128), 0).astype(f32)
        pick = jnp.zeros((1, 128), f32)
        for i in range(4):
            pick = pick + jnp.where(b == i, cnt[s, i : i + 1, :].astype(f32), 0.0)
        return jnp.where(at < pick, 1.0, 0.0)[:, 0:1]

    for s in range(3):
        r = pl.ds(s * T, T)
        v = nn(att[0, r, :], wblock(R["wo"])) + vec(V_OB) + rows[s].astype(f32)
        mid[r, :] = v
        n, _ = normalise(v)
        nbuf[s] = (n * vec(V_MG) + vec(V_MS)).astype(bf16)
        o = live_of(s) * cot[s].astype(f32)
        cot[s] = o.astype(bf16)
        part = col_sum(o)
        if s == 0:
            vg[V_DB : V_DB + 1, :] = part
        else:
            vg[V_DB : V_DB + 1, :] += part

    FT = FR

    def feed(res, gn2, n2t, tile):
        act_s, gh_s = tile.at[0], tile.at[1]
        for s in range(3):
            n2t[:, s * T : (s + 1) * T] = nbuf[s].T
        res[...] = jnp.zeros_like(res)
        gn2[...] = jnp.zeros_like(gn2)
        outer = branch = cot
        ub = R["ub"]

        @pl.loop(0, dps)
        def _(j):
            cols = ds128(j * FT, FT)
            up = wblock(R["wu"], cols)
            down = R["wd"][j]
            ub_j = ub[pl.ds(j, 1), :]

            @pl.loop(0, 3, init_carry=jnp.zeros((1, FT), f32))
            def bias_part(s, carry):
                r = slot_rows(s)
                hid = nn(nbuf[s], up) + ub_j
                phi_c = 0.5 * (1.0 + lax.erf(hid * 0.7071067811865476))
                act_low = (hid * phi_c).astype(bf16)
                act_s[r, :] = act_low
                res[r, :] += nn(act_low, down)
                slope = phi_c + hid * jnp.exp2(hid * hid * (-0.5 * LOG2E)) * 0.3989422804014327
                gh = (nt(outer[s], down) * slope).astype(bf16)
                gh_s[r, :] = gh
                gn2[r, :] += nt(gh, up)
                return carry + col_sum(gh.astype(f32))

            ub[pl.ds(j, 1), :] = bias_part
            R["wd"][j] = tn(act_s[...], outer[...].reshape(3 * T, W)).astype(bf16)
            R["wu"][:, :, cols] = nn(n2t[...], gh_s[...]).astype(bf16).reshape(dps, KR, FT)

        for s in range(3):
            r = pl.ds(s * T, T)
            v = mid[r, :]
            y = live_of(s) * (v + res[r, :] + vec(V_DB))
            n2t[r, :] = y.astype(bf16)
            move_home(s, n2t.at[r], act, S_ACT, I_ACT)
            n, inv = normalise(v)
            e_ = gn2[r, :]
            gm = outer[s].astype(f32) + norm_back(e_, n, inv, vec(V_MG))
            mid[r, :] = gm
            low = gm.astype(bf16)
            branch[s] = low
            for i, part in ((V_MG, col_sum(e_ * n)), (V_MS, col_sum(e_)), (V_OB, col_sum(low.astype(f32)))):
                if s == 0:
                    vg[i : i + 1, :] = part
                else:
                    vg[i : i + 1, :] += part
        if aligned:
            rs1(D_)
            rs1(U_)
        for s in range(3):
            r = pl.ds(s * T, T)
            nbuf[s] = nt(branch[s], wblock(R["wo"])).astype(bf16)
        send_do()
        for q in range(2):
            piece = tn(att[0, :, q * HALF : (q + 1) * HALF], branch[...].reshape(3 * T, W)).astype(bf16)
            R["wo"][q * (dps // 2) : (q + 1) * (dps // 2)] = piece.reshape(dps // 2, KR, W)
        for s in range(3):
            move_home_done(s, n2t.at[pl.ds(s * T, T)], act, S_ACT, I_ACT)

    do3 = R["nbuf"]

    def send_do(done=False):
        for j in range(2):
            i0 = EX["do"][0] if j == 0 else L0 + 4
            sref = do3.at[j, :, ds128(HALF * (1 - c), HALF)]
            dref = doa.at[ds128(2 * T * c + j * T, T)]
            d = rcopy(sref, dref, i0, i0, (other, z))
            d.wait_send() if done else d.start()
        for k in (1, 2, 3):
            t = lax.rem(g + k, 4)
            d = rcopy(
                do3.at[2, :, ds128(HALF * lax.div(t, 2) + 128 * lax.rem(t, 2), 256)],
                dob.at[ds128(T * g, T)],
                EX["do"][2] + k,
                EX["do"][1] + k,
                dev_of(t),
            )
            d.wait_send() if done else d.start()

    per = W // FT
    for q in range(dps):
        R["ub"][q : q + 1, :] = vt[V_UB + q // per : V_UB + q // per + 1, (q % per) * FT : (q % per + 1) * FT]
    pl.run_scoped(
        feed,
        pltpu.VMEM((3 * T, W), f32),
        pltpu.VMEM((3 * T, W), f32),
        pltpu.VMEM((W, 3 * T), bf16),
        pltpu.VMEM((2, 3 * T, FT), bf16),
    )
    for q in range(dps):
        vg[V_UB + q // per : V_UB + q // per + 1, (q % per) * FT : (q % per + 1) * FT] = R["ub"][q : q + 1, :]

    def grads_move(step):
        if not aligned:
            return
        if step == 0:
            rs1(O_)
            for a in (D_, U_, O_):
                rs2(a)
        elif step == 1:
            for a in (D_, U_, O_):
                rs3(a)
        elif step == 2:
            for a in (D_, U_, O_):
                rs4(a)
        elif step == 3:
            for a in (D_, U_, O_):
                y_send("QOUD"[a], 2)
        elif step == 4:
            for a in (D_, U_, O_):
                y_send("QOUD"[a], 3)
        elif step == 5:
            for a in (D_, U_, O_):
                y_final(a, outs[a])

    for j in range(2):
        doa[ds128(2 * T * c + j * T, T), :] = do3[j, :, ds128(HALF * c, HALF)]
    dob[ds128(T * g, T), :] = do3[2, :, ds128(HALF * e + 128 * c, 256)]
    recv(doa.at[ds128(2 * T * (1 - c), T)], EX["do"][0])
    recv(doa.at[ds128(2 * T * (1 - c) + T, T)], L0 + 4)
    grads_move(0)

    def attend_back(src, o_ref, d_ref, col, bi, sel, lrow, dk, dv, delta):
        cols = ds128(col, 128)
        k2 = src[1, :, cols]
        v2 = src[2, :, cols]
        kt = k2.T
        b = bias[bi]
        keys = [key_side(k2, b, i) for i in sel]
        dk[...] = jnp.zeros_like(dk)
        dv[...] = jnp.zeros_like(dv)
        prod = o_ref[0, :, cols].astype(f32) * d_ref[:, cols].astype(f32)
        hi = prod.astype(bf16)
        lo = (prod - hi.astype(f32)).astype(bf16)
        row = lax.broadcasted_iota(i32, (8, 128), 0)
        if len(sel) == 2:
            pickm = (row == lax.broadcasted_iota(i32, (8, 128), 1) // 64).astype(f32).astype(bf16)
        else:
            pickm = jnp.where(jnp.logical_and(row == 0, lane // 64 == sel[0]), 1.0, 0.0).astype(bf16)
        delta[...] = nt(pickm, hi) + nt(pickm, lo)

        @pl.loop(0, N // QT)
        def _(q):
            r = ds128(q * QT, QT)
            q2 = src[0, r, cols]
            d2 = d_ref[r, cols]
            dks, dvs, dqs = [], [], []
            for n, i in enumerate(sel):
                qm, dm = half(i, q2), half(i, d2)
                s = nt(keys[n], query_side(q2, i))
                p = jnp.exp2(s * SC - lse[pl.ds(lrow + n, 1), r])
                dp_ = nt(v2, dm)
                ds_ = (p * (dp_ - delta[pl.ds(n, 1), r])).astype(bf16)
                dvs.append(nn(p.astype(bf16), dm))
                dks.append(nn(ds_, qm))
                dqs.append(nn(kt, ds_).T if len(sel) == 1 else nn(kt[64 * i : 64 * i + 64], ds_))
            if len(sel) == 2:
                dk[...] += dks[0] + dks[1]
                dv[...] += dvs[0] + dvs[1]
                dq = jnp.concatenate(dqs, axis=0).T
            else:
                dk[...] += dks[0]
                dv[...] += dvs[0]
                dq = half(sel[0], dqs[0])
            src[0, r, cols] = (dq * 0.125).astype(bf16)

        src[1, :, cols] = (dk[...] * 0.125).astype(bf16)
        src[2, :, cols] = dv[...].astype(bf16)

    def back(dk, dv, delta):
        @pl.loop(0, 3)
        def _(t):
            attend_back(qkva, atta, doa, t * 128, 0, (0, 1), 2 * t, dk, dv, delta)

        from_heads_a("dqkv", qkva, qkv).start()
        from_heads_a_own("dqkv", qkva, qkv, L0 + 5).start()
        grads_move(1)
        for k in (1, 2, 3):
            recv(dob.at[ds128(T * lax.rem(g + 4 - k, 4), T)], EX["do"][1] + k)
        attend_back(qkvb, attb, dob, c * 128, 1, (0, 1), 6, dk, dv, delta)
        grads_move(2)
        attend_back(qkvb, attb, dob, (1 - c) * 128, 1, (c,), 8, dk, dv, delta)
        grads_move(3)

    pl.run_scoped(back, pltpu.VMEM((N, 128), f32), pltpu.VMEM((N, 128), f32), pltpu.VMEM((8, N), f32))
    xatt.wait_send()
    for d in xattb:
        d.wait_send()
    send_do(done=True)
    xb2 = [from_heads_b("dqkv", qkvb, 0, k) for k in (1, 2, 3)]
    for d in xb2:
        d.start()
    lb2 = from_heads_b_own(qkvb, L0 + 6)
    lb2.start()

    gsend = cot
    for s in range(3):
        normed_rows(s)

    def rows_back(s):
        r = pl.ds(s * T, T)
        e_ = nt(qkv[0, r, :], wblock(R["wq"], slice(0, W)))
        e_ += nt(qkv[1, r, :], wblock(R["wq"], slice(W, 2 * W)))
        e_ += nt(qkv[2, r, :], wblock(R["wq"], slice(2 * W, 3 * W)))
        n, inv = normalise(rows[s].astype(f32))
        gsend[s] = (mid[r, :] + norm_back(e_, n, inv, vec(V_NG))).astype(bf16)
        move_home(s, gsend.at[s], grh, S_GR, I_GR)
        parts = (
            (V_NG, col_sum(e_ * n)),
            (V_NS, col_sum(e_)),
            (V_QB, col_sum(qkv[0, r, :].astype(f32))),
            (V_VB, col_sum(qkv[2, r, :].astype(f32))),
        )
        for i, part in parts:
            if s == 0:
                vg[i : i + 1, :] = part
            else:
                vg[i : i + 1, :] += part

    for m in range(3):
        move_out_done(m, R["cnth"].at[m], cnt, S_CNT, I_CNT)
        move_out_done(m, R["cotangent"].at[m], cot, S_COT, I_COT)
    from_heads_a_own("dqkv", qkva, qkv, L0 + 5).wait()
    wait_a("dqkv", qkv, False)
    rows_back(0)
    rows_back(1)
    lb2.wait()
    wait_b_tokens("dqkv", 3)
    for j in range(3):
        merge_b(qkv, j, j)
    rows_back(2)
    for j in range(3):
        w = tn(nbuf[...].reshape(3 * T, W), qkv[j]).astype(bf16)
        R["wq"][:, :, j * W : (j + 1) * W] = w.reshape(dps, KR, W)
    if aligned:
        rs1(Q_)
        grads_move(4)
        rs2(Q_)
        grads_move(5)
        rs3(Q_)
        rs4(Q_)
        y_send("Q", 2)
        y_send("Q", 3)
        y_final(Q_, outs[Q_])
    else:
        save = [pltpu.make_async_copy(arrays[i], R[n], rs.at[L0 + 8 + i]) for i, n in enumerate(("gq", "go", "gu", "gd"))]
        for d in save:
            d.start()
        for d in save:
            d.wait()
    vg[12:16, :] = jnp.zeros((4, W), f32)
    from_heads_a("dqkv", qkva, qkv).wait_send()
    for d in xb2:
        d.wait_send()
    for s in range(3):
        move_home_done(s, gsend.at[s], grh, S_GR, I_GR)
    for m in range(3):
        arrived_home(m, act, I_ACT)
        arrived_home(m, grh, I_GR)
    assert count[0] <= cfg["sems"], count[0]


def scatter_kernel(keep, grads, out):
    places = lax.broadcasted_iota(i32, (out.shape[1], keep.shape[2]), 0)
    out[0] = nn((places == keep[0]).astype(f32).astype(bf16), grads[0])


def body(patches, keep_index, shard_counts, cotangent, *shards):
    ng, ns, wq, qb, vb, wo, ob, mg, ms, wu, ub, wd, db = shards
    batches, _, patch, width = patches.shape
    tokens = keep_index.shape[2]
    dp_size, blk_size = lax.axis_size("dp"), lax.axis_size("blk")
    devices = dp_size * blk_size
    ff = wu.shape[1]
    aligned = dp_size == 8 and blk_size == 4
    dps = 8
    kr, fr = width // dps, ff // dps
    vectors = jnp.stack([ng, ns, qb, vb, ob, mg, ms, db])
    if aligned:
        own = jnp.pad(vectors, ((0, 0), (0, 128 - vectors.shape[1])))
        own_ub = jnp.pad(ub[None], ((0, 7), (0, 128 - ub.shape[0])))
        table = jnp.concatenate([own, own_ub])
        weights = (wq, wo, wu, wd)
        pieces = [w.size // 128 for w in weights] + [16]
        flat = [sum(pieces[:i]) for i in range(6)]
    else:
        axes = ("dp", "blk")
        table = lax.all_gather(vectors, axes, axis=1, tiled=True).astype(f32)
        table_ub = lax.all_gather(ub, axes, axis=0, tiled=True).astype(f32).reshape(ff // width, width)
        table = jnp.concatenate([table, table_ub, jnp.zeros((16 - 8 - ff // width, width), f32)])
        weights = tuple(lax.all_gather(w, axes, axis=0, tiled=True) for w in (wq, wo, wu, wd))
        weights = tuple(w.reshape(dps, -1, w.shape[1]) for w in weights)
        flat = None
    cfg = dict(aligned=aligned, dps=dps, tokens=tokens, width=width, ff=ff, patch=patch, flat=flat, sems=260)
    keep = keep_index
    ins = [
        ("patches", patches[:, 0], ANY),
        ("keep", keep, VMEM),
        ("counts", shard_counts[:, 0], SMEM),
        ("cotangent", cotangent[:, 0], ANY),
    ]
    ins += [(n, w, VMEM if aligned else ANY) for n, w in zip(("sq", "so", "su", "sd"), weights)]
    ins.append(("sv", table, VMEM))
    out = [
        ("act", (3, tokens, width), bf16, ANY),
        ("grh", (3, tokens, width), bf16, ANY),
        ("vg", (16, width), f32, VMEM),
    ]
    full = {"q": (dps, kr, 3 * width), "o": (dps, kr, width), "u": (dps, kr, ff), "d": (dps, fr, width)}
    for i, n in enumerate("qoud"):
        if aligned:
            out.append(("g" + n, weights[i].shape, f32, VMEM))
        else:
            out.append(("g" + n, full[n], bf16, ANY))
    t3 = 3 * tokens
    scratch = [("w" + n, full[n], bf16) for n in "qoud"]
    scratch += [
        ("rows", (3, tokens, width), bf16),
        ("cot", (3, tokens, width), bf16),
        ("cnt", (3, 16, 128), bf16),
        ("cnth", (3, 16, 128), bf16),
        ("nbuf", (3, tokens, width), bf16),
        ("qkv", (3, t3, width), bf16),
        ("qkva", (3, 4 * tokens, width // 2), bf16),
        ("qkvb", (3, 4 * tokens, 256), bf16),
        ("atta", (1, 4 * tokens, width // 2), bf16),
        ("attb", (1, 4 * tokens, 256), bf16),
        ("att", (1, t3, width), bf16),
        ("fromb", (4, 3, tokens, 256), bf16),
        ("doa", (4 * tokens, width // 2), bf16),
        ("dob", (4 * tokens, 256), bf16),
        ("mid", (t3, width), f32),
        ("vt", (16, width), f32),
        ("lse", (16, 4 * tokens), f32),
        ("bias", (2, 4 * tokens, 128), bf16),
        ("ub", (dps, fr), f32),
    ]
    if aligned:
        scratch += [
            ("zbuf", (4, flat[5], 128), bf16),
            ("zrr", (3, flat[4], 128), bf16),
            ("zrl", (3, flat[4], 128), bf16),
            ("vw", (dps, 64, 128), bf16),
        ]
        scratch += [("rb1" + n, (4, *full[n][1:]), bf16) for n in "qoud"]
        scratch += [("rb2" + n, (3, *full[n][1:]), bf16) for n in "qoud"]
    names = [n for n, _, _ in scratch] + ["ss", "rs"]
    shapes = [pltpu.VMEM(s, d) for _, s, d in scratch] + [pltpu.SemaphoreType.DMA((cfg["sems"],))] * 2
    flops = 6 * 3 * tokens * (4 * width * width + 2 * width * ff)
    results = pl.pallas_call(
        functools.partial(layer_kernel, cfg, [n for n, _, _ in ins], [n for n, *_ in out], names),
        out_shape=[jax.ShapeDtypeStruct(s, d) for _, s, d, _ in out],
        in_specs=[s for _, _, s in ins],
        out_specs=[s for *_, s in out],
        scratch_shapes=shapes,
        compiler_params=pltpu.CompilerParams(collective_id=0, has_side_effects=True, vmem_limit_bytes=64 * 1024 * 1024 - 512 * 1024),
        cost_estimate=pl.CostEstimate(flops=flops, bytes_accessed=50_000_000, transcendentals=0),
        name="layer",
    )(*[a for _, a, _ in ins])
    act, grh, vg, gq, go, gu, gd = results
    patch_grad = pl.pallas_call(
        scatter_kernel,
        grid=(3,),
        in_specs=[pl.BlockSpec((1, 1, tokens), lambda m: (m, 0, 0)), pl.BlockSpec((1, tokens, width), lambda m: (m, 0, 0))],
        out_specs=pl.BlockSpec((1, patch, width), lambda m: (m, 0, 0)),
        out_shape=jax.ShapeDtypeStruct((3, patch, width), f32),
        compiler_params=pltpu.CompilerParams(vmem_limit_bytes=32 * 1024 * 1024),
        name="scatter",
    )(keep, grh)
    small = jnp.concatenate([vg[:8].reshape(8, devices, -1).transpose(1, 0, 2).reshape(devices, -1), vg[8 : 8 + ff // width].reshape(devices, -1)], axis=1)
    small = lax.psum_scatter(small, ("dp", "blk"), scatter_dimension=0, tiled=True)[0]
    n = width // devices
    piece = [small[i * n : (i + 1) * n] for i in range(8)] + [small[8 * n :]]
    if not aligned:
        axes = ("dp", "blk")
        gq, go, gu, gd = (
            lax.psum_scatter(w.reshape(-1, w.shape[-1]).astype(f32), axes, scatter_dimension=0, tiled=True) for w in (gq, go, gu, gd)
        )
    return (
        act[:, None],
        patch_grad[:, None],
        piece[V_NG],
        piece[V_NS],
        gq,
        piece[V_QB],
        piece[V_VB],
        go,
        piece[V_OB],
        piece[V_MG],
        piece[V_MS],
        gu,
        piece[V_UB],
        gd,
        piece[V_DB],
    )


def solution(mesh):
    vec, mat = P(("dp", "blk")), P(("dp", "blk"), None)
    tok = P(None, "dp", "blk", None)
    params = (vec, vec, mat, vec, vec, mat, vec, vec, vec, mat, vec, mat, vec)
    in_specs = (tok, P(None, "dp", "blk"), P(None, "dp", None), tok) + params
    out_specs = (tok, tok) + params
    return jax.shard_map(body, mesh=mesh, in_specs=in_specs, out_specs=out_specs, check_vma=False)
```

time: 1250 us -> 403 us (0.32)
  waiting for transfers between devices: 596 us -> 0 us
  Pallas kernels: 0 us -> 340 us
  matrix products: 309 us -> 0 us
  blocking collectives: 165 us -> 45.2 us
  local copies, waits for them, and re-layouts: 84.9 us -> 10.2 us
  other arithmetic: 59.8 us -> 1.33 us
  between operations: 17.7 us -> 1.16 us
    pallas_call x0 -> x2, Pallas kernels: none -> 340 us  [the longest x1 337 us: body(): pl.pallas_call(functools.partial(layer_kernel, cfg, [n for n, _, _ in ins...]
    reduce_scatter x4 -> x0, waiting for transfers between devices: 322 us -> none  [body(): lax.psum_scatter(totals, ('dp', 'blk'), scatter_dimension=0, tiled=True)]
    dot_general x57 -> x0, matrix products: 309 us -> none  [the longest x12 47.2 us: inner_rows(): lax.dot_general(left, right, (((0,), (0,)), ((), ())), preferred_element_...]
    all_gather x16 -> x0, waiting for transfers between devices: 270 us -> none  [the longest x3 69.1 us: body(): lax.all_gather(values_low, 'blk', axis=0, tiled=True)]
    all_gather x6 -> x0, blocking collectives: 69.1 us -> none  [the longest x3 35 us: body(): lax.all_gather(row_total, 'blk', axis=1, tiled=True)]
    unnamed x2 -> x1, blocking collectives: 96.2 us -> 45.2 us
    unnamed x509 -> x20, local copies, waits for them, and re-layouts: 37.3 us -> 6.37 us
    all_gather x12 -> x0, local copies, waits for them, and re-layouts: 27.1 us -> none  [the longest x3 7.82 us: body(): lax.all_gather(values_low, 'blk', axis=0, tiled=True)]
  transfers between devices with their start and end apart: 20 -> 0, of which waited for: 12 -> 0; matrix products, arithmetic and copies ran while one was open for 34% -> 0% of each run, Pallas kernels for 0% -> 0%
where the time goes in v1:
time: 403 us; the launch traced here: 398 us
  Pallas kernels  340 us (84%)
  blocking collectives  45.2 us (11%)
  local copies, waits for them, and re-layouts  10.2 us (3%)
    pallas_call x1, Pallas kernels, body(): pl.pallas_call(functools.partial(layer_kernel, cfg, [n for n, _, _ in ins...  337 us
    unnamed x1, blocking collectives  45.2 us

profile of v1, /device:TPU:5, one launch (start us, length us, event | category | flops | bytes accessed | tf_op | source)
XLA Modules:
  0.0 398.3 jit_solution(13599570950186070567)
XLA Ops:
  0.6 1.3 copy.43
  1.9 0.8 stack.35
  2.7 1.3 fusion.2.refs_8_
  4.0 0.0 copy-start.1
  4.0 337.3 %layer.1 = (bf16[3,256,768]{2,1,0:T(8,128)(2,1)}, bf16[3,256,768]{2,1,0:T(8,128)(2,1)}, f32[16,768]{1,0:T(8,128)}, f32[24,2304]{1,0:T(8,128)}, f32[24,768]{1,0:T...) custom-call(bf16[3,512,768]{2,1,0:T(8,128)(2,1)} %bitcast.52, s32[3,1,256]{2,1,0:T(1,128)} %keep.1, s32[3,4]{1,0:T(4,128)} %bitcast.42, ...), custom_call_target="tpu_custom_call" | custom-call | flops 32614907904 | bytes 50000000 | tf_op jit(solution)/shard_map/layer/pallas_call | solution.py:1103
  341.3 0.7 slice.61
  342.0 0.7 slice.60
  342.7 0.1 reshape.50
  342.8 0.1 reshape.48
  342.9 0.1 copy.38
  343.0 0.1 reshape.49
  343.1 0.1 pad_maximum_fusion
  343.2 45.2 %all-reduce.2 = f32[32,288]{1,0:T(8,128)S(1)} all-reduce(f32[32,288]{1,0:T(8,128)S(1)} %pad_maximum_fusion), channel_id=2, replica_groups=mesh['dp'=8,'blk'=4] {'dp','blk'}, use_global_device_ids=true, to_apply=%region_0.1.clone | all-reduce | flops 9216 | bytes 73728
  388.4 0.6 dynamic-slice_bitcast_fusion.1
  389.0 0.6 dynamic-slice_bitcast_fusion
  389.6 0.0 copy-done.1
  389.6 0.0 copy-start
  389.6 1.3 copy-done
  390.9 0.0 copy-start.2
  390.9 3.1 scatter.1
  394.0 0.0 copy-done.2
  394.0 0.0 copy-start.5
  394.0 0.0 copy-start.6
  394.0 0.0 copy-start.4
  394.0 0.0 copy-start.3
  394.0 1.0 copy.49
  395.0 0.1 copy-done.5
  395.1 0.7 copy.50
  395.7 0.0 copy-done.6
  395.8 0.6 copy.51
  396.4 0.0 copy-done.4
  396.4 0.7 copy.52
  397.1 0.0 copy-done.3
  397.1 0.7 copy.53
Async XLA Ops:
  4.0 385.7 %copy-start.1 = (s32[3,1,256]{2,1,0:T(1,128)S(1)}, s32[3,1,256]{2,1,0:T(1,128)}, u32[]{:S(2)}) copy-start(s32[3,1,256]{2,1,0:T(1,128)} %keep.1) | copy-start | bytes 9220
  389.6 1.3 copy-start
  390.9 3.1 copy-start.2
  394.0 1.1 copy-start.5
  394.0 1.8 copy-start.6
  394.0 2.4 copy-start.4
  394.0 3.1 copy-start.3

commit v2 on v1

--- a/solution.py
+++ b/solution.py
@@ -161,16 +161,22 @@
     if aligned:
         zbuf, zrr, zrl = R["zbuf"], R["zrr"], R["zrl"]
         flat = cfg["flat"]
-        CH = {"Q": (0, flat[1]), "O": (flat[1], flat[2]), "U": (flat[2], flat[3]), "D": (flat[3], flat[4]), "V": (flat[4], flat[5])}
+        CH = {"Q": (0, flat[1]), "OU": (flat[1], flat[3]), "D": (flat[3], flat[4]), "V": (flat[4], flat[5])}
         ZR = {k: take(3) - 1 for k in CH}
         ZL = {k: take(3) - 1 for k in CH}
-        YR = {k: take(3) - 1 for k in "QOUD"}
-        YL = {k: take(3) - 1 for k in "QOUD"}
+        wide = W // 128
+        GC = {"D": (D_, 0, wide), "O": (O_, 0, wide)}
+        for i in range(2):
+            GC["U%d" % i] = (U_, i * F // 256, (i + 1) * F // 256)
+        for i in range(3):
+            GC["Q%d" % i] = (Q_, i * wide, (i + 1) * wide)
+        YR = {k: take(3) - 1 for k in GC}
+        YL = {k: take(3) - 1 for k in GC}
         gathered = arrays + [R["vw"]]
         XY = [take(3) for _ in range(5)]
         CR = [take(4) for _ in range(5)]
-        R1 = [take(4) for _ in range(4)]
-        R2 = [take(3) for _ in range(4)]
+        R1 = {k: take(4) for k in GC}
+        R2 = {k: take(3) for k in GC}
 
         def z_send(key, k, done=False):
             r0, r1 = CH[key]
@@ -202,7 +208,7 @@
             def _():
                 recv(zbuf.at[z + k, rows], ZL[key] + k)
 
-        def flatten(a, ref, slot, block=None):
+        def flatten(a, ref, slot):
             if a == D_:
                 n, rows = W // 128, FR // 4
             elif a == 4:
@@ -211,8 +217,7 @@
                 n, rows = ref.shape[-1] // 128, KR // 4
             for t in range(n):
                 cols = slice(t * 128, (t + 1) * 128)
-                piece = ref[:, cols] if block is None else ref[block, slot * rows : (slot + 1) * rows, cols]
-                zbuf[slot, flat[a] + t * rows : flat[a] + (t + 1) * rows, :] = piece
+                zbuf[slot, flat[a] + t * rows : flat[a] + (t + 1) * rows, :] = ref[:, cols]
 
         def unflatten(a, block):
             dst = gathered[a]
@@ -276,61 +281,84 @@
         bufs1 = [R["rb1" + n] for n in "qoud"]
         bufs2 = [R["rb2" + n] for n in "qoud"]
 
-        def view(buf, a, i):
-            r, w = arrays[a].shape[1:]
-            return buf.at[i, pl.ds(0, r), pl.ds(0, w)]
-
-        def rs_core(a, i):
-            return rcopy(arrays[a].at[2 * i + 1 - c], view(bufs1[a], a, i), R1[a] + i, R1[a] + i, (other, z))
-
-        def rs1(a):
+        def cols_of(key):
+            _, t0, t1 = GC[key]
+            return pl.ds(t0 * 128, (t1 - t0) * 128)
+
+        def block_of(key, block):
+            return arrays[GC[key][0]].at[block, :, cols_of(key)]
+
+        def view(bufs, key, i):
+            return bufs[GC[key][0]].at[i, :, cols_of(key)]
+
+        def rs_core(key, i):
+            return rcopy(block_of(key, 2 * i + 1 - c), view(bufs1, key, i), R1[key] + i, R1[key] + i, (other, z))
+
+        def rs1(key):
             for i in range(4):
-                rs_core(a, i).start()
-
-        def addto(ref, block, parts):
-            rows, width = ref.shape[1:]
-            step = 96
+                rs_core(key, i).start()
+
+        def addto(key, block, parts):
+            ref, cols = arrays[GC[key][0]], cols_of(key)
+            rows = ref.shape[1]
+            step = 48
 
             @pl.loop(0, rows // step)
             def _(q):
                 r = pl.ds(mult(q * step, step), step)
-                total = ref[block, r, :].astype(f32)
+                total = ref[block, r, cols].astype(f32)
                 for p, i in parts:
-                    total = total + p[i, r, pl.ds(0, width)].astype(f32)
-                ref[block, r, :] = total.astype(bf16)
-
-        def rs_xy(a):
-            ref = arrays[a]
+                    total = total + p[GC[key][0]][i, r, cols].astype(f32)
+                ref[block, r, cols] = total.astype(bf16)
+
+        def rs_xy(key):
+            i0 = R2[key]
             return {
-                "diag": lambda: rcopy(ref.at[p3], view(bufs2[a], a, 0), R2[a], R2[a], (p2, z)),
-                "p2": lambda: rcopy(ref.at[p2], view(bufs2[a], a, 1), R2[a] + 1, R2[a] + 1, (p2, z)),
-                "p1": lambda: rcopy(ref.at[p1], view(bufs2[a], a, 2), R2[a] + 2, R2[a] + 2, (p1, z)),
+                "diag": lambda: rcopy(block_of(key, p3), view(bufs2, key, 0), i0, i0, (p2, z)),
+                "p2": lambda: rcopy(block_of(key, p2), view(bufs2, key, 1), i0 + 1, i0 + 1, (p2, z)),
+                "p1": lambda: rcopy(block_of(key, p1), view(bufs2, key, 2), i0 + 2, i0 + 2, (p1, z)),
             }
 
-        def rs2(a):
+        def rs2_pair(key, i):
+            recv(view(bufs1, key, i), R1[key] + i)
+            addto(key, blk_of(i), [(bufs1, i)])
+
+            @pl.when(blk_of(i) == p3)
+            def _():
+                rs_xy(key)["diag"]().start()
+
+            @pl.when(blk_of(i) == p2)
+            def _():
+                rs_xy(key)["p2"]().start()
+
+        def rs2(key):
             for i in range(4):
-                recv(view(bufs1[a], a, i), R1[a] + i)
-                addto(arrays[a], blk_of(i), [(bufs1[a], i)])
-            d = rs_xy(a)
-            d["diag"]().start()
-            d["p2"]().start()
-
-        def rs3(a):
-            recv(view(bufs2[a], a, 0), R2[a])
-            addto(arrays[a], p1, [(bufs2[a], 0)])
-            rs_xy(a)["p1"]().start()
-
-        def rs4(a):
-            recv(view(bufs2[a], a, 1), R2[a] + 1)
-            recv(view(bufs2[a], a, 2), R2[a] + 2)
-            addto(arrays[a], dp, [(bufs2[a], 1), (bufs2[a], 2)])
-            for s in range(4):
-                flatten(a, arrays[a], s, dp)
-            y_send("QOUD"[a], 1)
+                rs2_pair(key, i)
+
+        def rs3(key):
+            recv(view(bufs2, key, 0), R2[key])
+            addto(key, p1, [(bufs2, 0)])
+            rs_xy(key)["p1"]().start()
+
+        def span(key):
+            a, t0, t1 = GC[key]
+            n = arrays[a].shape[1] // 4
+            return a, n, flat[a] + t0 * n, (t1 - t0) * n
+
+        def rs4(key):
+            recv(view(bufs2, key, 1), R2[key] + 1)
+            recv(view(bufs2, key, 2), R2[key] + 2)
+            addto(key, dp, [(bufs2, 1), (bufs2, 2)])
+            a, n, _, _ = span(key)
+            for slot in range(4):
+                for t in range(GC[key][1], GC[key][2]):
+                    piece = arrays[a][dp, slot * n : (slot + 1) * n, t * 128 : (t + 1) * 128]
+                    zbuf[slot, flat[a] + t * n : flat[a] + (t + 1) * n, :] = piece
+            y_send(key, 1)
 
         def y_send(key, k, done=False):
-            r0, r1 = CH[key]
-            rows = pl.ds(r0, r1 - r0)
+            _, _, r0, rn = span(key)
+            rows = pl.ds(r0, rn)
             to_right = z + 4 - k
             to_left = z - 4 + k
 
@@ -358,10 +386,9 @@
                 d = rcopy(zbuf.at[to_left, rows], zrl.at[k - 1, rows], YL[key] + k, YL[key] + k, (dp, z - 1))
                 d.wait_send() if done else d.start()
 
-        def y_final(a, out):
-            key = "QOUD"[a]
-            r0, r1 = CH[key]
-            rows = pl.ds(r0, r1 - r0)
+        def y_final(key):
+            a, n, r0, rn = span(key)
+            rows = pl.ds(r0, rn)
 
             @pl.when(z >= 1)
             def _():
@@ -371,21 +398,19 @@
             def _():
                 recv(zrl.at[2, rows], YL[key] + 3)
 
-            if a == D_:
-                n, step = W // 128, FR // 4
-            else:
-                n, step = out.shape[-1] // 128, KR // 4
-            for t in range(n):
-                piece = slice(r0 + t * step, r0 + (t + 1) * step)
+            for t in range(GC[key][1], GC[key][2]):
+                piece = slice(flat[a] + t * n, flat[a] + (t + 1) * n)
                 total = zbuf[z, piece, :].astype(f32)
                 total = total + jnp.where(z >= 1, zrr[2, piece, :].astype(f32), 0.0)
                 total = total + jnp.where(z <= 2, zrl[2, piece, :].astype(f32), 0.0)
-                out[:, t * 128 : (t + 1) * 128] = total
+                outs[a][:, t * 128 : (t + 1) * 128] = total
+
+        def rs_done(key):
             for k in (1, 2, 3):
                 y_send(key, k, done=True)
             for i in range(4):
-                rs_core(a, i).wait_send()
-            for d in rs_xy(a).values():
+                rs_core(key, i).wait_send()
+            for d in rs_xy(key).values():
                 d().wait_send()
 
         outs = [R["gq"], R["go"], R["gu"], R["gd"]]
@@ -412,48 +437,63 @@
             R["cnth"][m, b : b + 1, :] = jnp.full((1, 128), R["counts"][m, b], i32).astype(f32).astype(bf16)
         R["cnth"][m, 4:, :] = jnp.zeros((12, 128), bf16)
 
-    pl.semaphore_wait(bar, len(peers))
-    if aligned:
-        z_send("Q", 1)
-        z_send("V", 1)
-
     def pick_rows(pbuf, psem):
         copies = [pltpu.make_async_copy(R["patches"].at[m], pbuf.at[m], psem.at[m]) for m in range(3)]
         for d in copies:
             d.start()
+        pl.semaphore_wait(bar, len(peers))
+        if aligned:
+            z_send("Q", 1)
+            z_send("V", 1)
         for m in range(3):
             copies[m].wait()
             spread = (lax.broadcasted_iota(i32, (cfg["patch"], T), 0) == keep[m]).astype(f32).astype(bf16)
             att[0, m * T : (m + 1) * T, :] = tn(spread, pbuf[m]).astype(bf16)
+
+    pl.run_scoped(pick_rows, pltpu.VMEM((3, cfg["patch"], W), bf16), pltpu.SemaphoreType.DMA((3,)))
+
+    def send_rows():
+        for m in (2, 0, 1):
             move_out(m, att.at[0, pl.ds(m * T, T)], rows, S_ROWS, I_ROWS)
             move_out(m, R["cnth"].at[m], cnt, S_CNT, I_CNT)
 
-    pl.run_scoped(pick_rows, pltpu.VMEM((3, cfg["patch"], W), bf16), pltpu.SemaphoreType.DMA((3,)))
+    def send_cot():
+        for m in (2, 0, 1):
+            move_out(m, R["cotangent"].at[m], cot, S_COT, I_COT)
+
     if aligned:
-        for k in (1, 2):
-            for key in "QV":
-                z_wait(key, k)
-                z_send(key, k + 1)
-        for key in "OUD":
-            z_send(key, 1)
+        for key in "QV":
+            z_wait(key, 1)
+            z_send(key, 2)
+        z_send("OU", 1)
+        for key in "QV":
+            z_wait(key, 2)
+            z_send(key, 3)
+        z_wait("OU", 1)
+        z_send("OU", 2)
         for key in "QV":
             z_wait(key, 3)
         unflatten(Q_, dp)
         ag1(Q_)
         unflatten(4, dp)
         ag1(4)
+        z_wait("OU", 2)
+        z_send("OU", 3)
+        send_rows()
+        z_send("D", 1)
     else:
         full = [pltpu.make_async_copy(R[n], arrays[i], rs.at[L0 + 8 + i]) for i, n in enumerate(("sq", "so", "su", "sd"))]
         for d in full:
             d.start()
-    for m in range(3):
-        move_out(m, R["cotangent"].at[m], cot, S_COT, I_COT)
+        send_rows()
+        send_cot()
     if aligned:
         ag2(Q_)
         ag2(4)
-        for key in "OUD":
-            z_wait(key, 1)
-            z_send(key, 2)
+        z_wait("OU", 3)
+        for a in (U_, O_):
+            unflatten(a, dp)
+            ag1(a)
         ag3(Q_)
         ag3(4)
         ag4(4)
@@ -481,18 +521,16 @@
         n, _ = normalise(rows[s].astype(f32))
         nbuf[s] = (n * vec(V_NG) + vec(V_NS)).astype(bf16)
 
-    for s in range(3):
+    for s in (2, 0, 1):
         recv(rows.at[s], I_ROWS + s)
         recv(cnt.at[s], I_CNT + s)
         normed_rows(s)
-    if aligned:
-        ag4(Q_)
-        for key in "OUD":
-            z_wait(key, 2)
-            z_send(key, 3)
-    else:
-        for d in full:
-            d.wait()
+        if s == 2:
+            if aligned:
+                ag4(Q_)
+            else:
+                for d in full:
+                    d.wait()
 
     def wblock(ref, cols=None):
         v = ref[...] if cols is None else ref[:, :, cols]
@@ -590,16 +628,8 @@
             dst[j, 2 * T : 3 * T, at + 128 : at + 256] = jnp.where(lane < 64, lo[:, 128:256], hi[:, 0:128])
             dst[j, 2 * T : 3 * T, at + 256 : at + 384] = hi[:, 128:256]
 
-    @pl.loop(0, 2)
-    def _(s):
-        project(s)
-
     for m in range(3):
         move_out_done(m, att.at[0, pl.ds(m * T, T)], rows, S_ROWS, I_ROWS)
-    xa = to_heads_a("qkv", qkv, qkva)
-    xa.start()
-    la = to_heads_a_own("qkv", qkv, qkva, L0)
-    la.start()
     project(2)
     xb = [to_heads_b("qkv", qkv, qkvb, k) for k in (1, 2, 3)]
     for d in xb:
@@ -607,24 +637,42 @@
     lb = to_heads_b_own("qkv", qkv, qkvb, L0 + 1)
     lb.start()
 
+    @pl.loop(0, 2)
+    def _(s):
+        project(s)
+
+    xa = to_heads_a("qkv", qkv, qkva)
+    xa.start()
+    la = to_heads_a_own("qkv", qkv, qkva, L0)
+    la.start()
+
     def weights_ready(step):
         if not aligned:
             return
         if step == 0:
-            for key in "OUD":
-                z_wait(key, 3)
-            for a in (O_, U_, D_):
-                unflatten(a, dp)
-                ag1(a)
+            z_wait("D", 1)
+            z_send("D", 2)
+            for a in (U_, O_):
+                ag2(a)
         elif step == 1:
-            for a in (O_, U_, D_):
-                ag2(a)
+            z_wait("D", 2)
+            z_send("D", 3)
+            send_cot()
+            for a in (U_, O_):
+                ag3(a)
         elif step == 2:
-            for a in (O_, U_, D_):
-                ag3(a)
+            z_wait("D", 3)
+            unflatten(D_, dp)
+            ag1(D_)
         elif step == 3:
-            for a in (O_, U_, D_):
+            ag2(D_)
+        elif step == 4:
+            for a in (U_, O_):
                 ag4(a)
+        elif step == 5:
+            ag3(D_)
+        elif step == 6:
+            ag4(D_)
             for key in CH:
                 for k in (1, 2, 3):
                     z_send(key, k, done=True)
@@ -685,42 +733,32 @@
     la.wait()
     wait_a("qkv", qkva, True)
 
-    @pl.loop(0, 2)
-    def _(t):
+    for t in range(3):
         attend(qkva, atta, t * 128, 0, (0, 1), 2 * t)
-
-    weights_ready(0)
-    attend(qkva, atta, 256, 0, (0, 1), 4)
+        weights_ready(t)
     xatt = from_heads_a("att", atta, att)
     xatt.start()
     latt = from_heads_a_own("att", atta, att, L0 + 2)
     latt.start()
     lb.wait()
     wait_b_heads("qkv", qkvb)
-    weights_ready(1)
     attend(qkvb, attb, c * 128, 1, (0, 1), 6)
-    weights_ready(2)
+    weights_ready(3)
     attend(qkvb, attb, (1 - c) * 128, 1, (c,), 8)
     xattb = [from_heads_b("att", attb, 0, k) for k in (1, 2, 3)]
     for d in xattb:
         d.start()
     lattb = from_heads_b_own(attb, L0 + 3)
     lattb.start()
-    weights_ready(3)
+    weights_ready(4)
     xa.wait_send()
     for d in xb:
         d.wait_send()
     latt.wait()
     wait_a("att", att, False)
-    lattb.wait()
-    wait_b_tokens("att", 1)
-    merge_b(att, 0, 0)
 
     def slot_rows(s):
         return pl.ds(mult(s * T, T), T)
-
-    for s in range(3):
-        recv(cot.at[s], I_COT + s)
 
     def live_of(s):
         b = 2 * c + s if s < 2 else g
@@ -731,15 +769,23 @@
         return jnp.where(at < pick, 1.0, 0.0)[:, 0:1]
 
     for s in range(3):
+        if s == 2:
+            lattb.wait()
+            wait_b_tokens("att", 1)
+            merge_b(att, 0, 0)
+            weights_ready(5)
         r = pl.ds(s * T, T)
         v = nn(att[0, r, :], wblock(R["wo"])) + vec(V_OB) + rows[s].astype(f32)
         mid[r, :] = v
         n, _ = normalise(v)
         nbuf[s] = (n * vec(V_MG) + vec(V_MS)).astype(bf16)
+    weights_ready(6)
+    for s in (2, 0, 1):
+        recv(cot.at[s], I_COT + s)
         o = live_of(s) * cot[s].astype(f32)
         cot[s] = o.astype(bf16)
         part = col_sum(o)
-        if s == 0:
+        if s == 2:
             vg[V_DB : V_DB + 1, :] = part
         else:
             vg[V_DB : V_DB + 1, :] += part
@@ -755,8 +801,12 @@
         outer = branch = cot
         ub = R["ub"]
 
-        @pl.loop(0, dps)
-        def _(j):
+        def tile_pair(i):
+            @pl.loop(2 * i, 2 * i + 2)
+            def _(j):
+                one_tile(j)
+
+        def one_tile(j):
             cols = ds128(j * FT, FT)
             up = wblock(R["wu"], cols)
             down = R["wd"][j]
@@ -780,12 +830,22 @@
             R["wd"][j] = tn(act_s[...], outer[...].reshape(3 * T, W)).astype(bf16)
             R["wu"][:, :, cols] = nn(n2t[...], gh_s[...]).astype(bf16).reshape(dps, KR, FT)
 
-        for s in range(3):
+        for i in range(dps // 2):
+            tile_pair(i)
+            if aligned:
+                rs_core("D", i).start()
+                if i == 1 or i == 3:
+                    rs1("U%d" % (i // 2))
+                if i > 0:
+                    rs2_pair("D", i - 1)
+                if i == 2:
+                    rs2("U0")
+
+        for s in (2, 0, 1):
             r = pl.ds(s * T, T)
             v = mid[r, :]
             y = live_of(s) * (v + res[r, :] + vec(V_DB))
             n2t[r, :] = y.astype(bf16)
-            move_home(s, n2t.at[r], act, S_ACT, I_ACT)
             n, inv = normalise(v)
             e_ = gn2[r, :]
             gm = outer[s].astype(f32) + norm_back(e_, n, inv, vec(V_MG))
@@ -793,42 +853,75 @@
             low = gm.astype(bf16)
             branch[s] = low
             for i, part in ((V_MG, col_sum(e_ * n)), (V_MS, col_sum(e_)), (V_OB, col_sum(low.astype(f32)))):
-                if s == 0:
+                if s == 2:
                     vg[i : i + 1, :] = part
                 else:
                     vg[i : i + 1, :] += part
-        if aligned:
-            rs1(D_)
-            rs1(U_)
-        for s in range(3):
-            r = pl.ds(s * T, T)
-            nbuf[s] = nt(branch[s], wblock(R["wo"])).astype(bf16)
-        send_do()
+            nbuf[s] = nt(low, wblock(R["wo"])).astype(bf16)
+            send_do(s)
         for q in range(2):
             piece = tn(att[0, :, q * HALF : (q + 1) * HALF], branch[...].reshape(3 * T, W)).astype(bf16)
             R["wo"][q * (dps // 2) : (q + 1) * (dps // 2)] = piece.reshape(dps // 2, KR, W)
+        att[0] = n2t[...]
+        for s in (2, 0, 1):
+            move_home(s, att.at[0, pl.ds(s * T, T)], act, S_ACT, I_ACT)
+        grads_move(0)
+
+    def act_done():
         for s in range(3):
-            move_home_done(s, n2t.at[pl.ds(s * T, T)], act, S_ACT, I_ACT)
+            move_home_done(s, att.at[0, pl.ds(s * T, T)], act, S_ACT, I_ACT)
 
     do3 = R["nbuf"]
 
-    def send_do(done=False):
-        for j in range(2):
-            i0 = EX["do"][0] if j == 0 else L0 + 4
-            sref = do3.at[j, :, ds128(HALF * (1 - c), HALF)]
-            dref = doa.at[ds128(2 * T * c + j * T, T)]
-            d = rcopy(sref, dref, i0, i0, (other, z))
-            d.wait_send() if done else d.start()
+    def do_copies(s):
+        if s < 2:
+            i0 = EX["do"][0] if s == 0 else L0 + 4
+            return [rcopy(do3.at[s, :, ds128(HALF * (1 - c), HALF)], doa.at[ds128(2 * T * c + s * T, T)], i0, i0, (other, z))]
+        out = []
         for k in (1, 2, 3):
             t = lax.rem(g + k, 4)
-            d = rcopy(
-                do3.at[2, :, ds128(HALF * lax.div(t, 2) + 128 * lax.rem(t, 2), 256)],
-                dob.at[ds128(T * g, T)],
-                EX["do"][2] + k,
-                EX["do"][1] + k,
-                dev_of(t),
-            )
-            d.wait_send() if done else d.start()
+            cols = ds128(HALF * lax.div(t, 2) + 128 * lax.rem(t, 2), 256)
+            out.append(rcopy(do3.at[2, :, cols], dob.at[ds128(T * g, T)], EX["do"][2] + k, EX["do"][1] + k, dev_of(t)))
+        return out
+
+    def send_do(s):
+        for d in do_copies(s):
+            d.start()
+
+    def grads_move(step):
+        if not aligned:
+            return
+        if step == 0:
+            rs1("O")
+            rs2_pair("D", 3)
+            rs3("U0")
+            rs2("U1")
+            rs3("D")
+        elif step == 1:
+            rs2("O")
+            rs4("U0")
+            rs3("U1")
+        elif step == 2:
+            rs4("D")
+            rs3("O")
+            y_send("U0", 2)
+        elif step == 3:
+            rs4("U1")
+            y_send("D", 2)
+            y_send("U0", 3)
+        elif step == 4:
+            rs4("O")
+            y_send("D", 3)
+            y_send("U1", 2)
+            y_final("U0")
+        elif step == 5:
+            y_send("O", 2)
+            y_send("U1", 3)
+            y_final("D")
+        elif step == 6:
+            y_send("O", 3)
+            y_final("U1")
+            y_final("O")
 
     per = W // FT
     for q in range(dps):
@@ -843,35 +936,11 @@
     for q in range(dps):
         vg[V_UB + q // per : V_UB + q // per + 1, (q % per) * FT : (q % per + 1) * FT] = R["ub"][q : q + 1, :]
 
-    def grads_move(step):
-        if not aligned:
-            return
-        if step == 0:
-            rs1(O_)
-            for a in (D_, U_, O_):
-                rs2(a)
-        elif step == 1:
-            for a in (D_, U_, O_):
-                rs3(a)
-        elif step == 2:
-            for a in (D_, U_, O_):
-                rs4(a)
-        elif step == 3:
-            for a in (D_, U_, O_):
-                y_send("QOUD"[a], 2)
-        elif step == 4:
-            for a in (D_, U_, O_):
-                y_send("QOUD"[a], 3)
-        elif step == 5:
-            for a in (D_, U_, O_):
-                y_final(a, outs[a])
-
     for j in range(2):
         doa[ds128(2 * T * c + j * T, T), :] = do3[j, :, ds128(HALF * c, HALF)]
     dob[ds128(T * g, T), :] = do3[2, :, ds128(HALF * e + 128 * c, 256)]
     recv(doa.at[ds128(2 * T * (1 - c), T)], EX["do"][0])
     recv(doa.at[ds128(2 * T * (1 - c) + T, T)], L0 + 4)
-    grads_move(0)
 
     def attend_back(src, o_ref, d_ref, col, bi, sel, lrow, dk, dv, delta):
         cols = ds128(col, 128)
@@ -921,40 +990,46 @@
         src[2, :, cols] = dv[...].astype(bf16)
 
     def back(dk, dv, delta):
-        @pl.loop(0, 3)
-        def _(t):
-            attend_back(qkva, atta, doa, t * 128, 0, (0, 1), 2 * t, dk, dv, delta)
-
-        from_heads_a("dqkv", qkva, qkv).start()
-        from_heads_a_own("dqkv", qkva, qkv, L0 + 5).start()
+        attend_back(qkva, atta, doa, 0, 0, (0, 1), 0, dk, dv, delta)
         grads_move(1)
         for k in (1, 2, 3):
             recv(dob.at[ds128(T * lax.rem(g + 4 - k, 4), T)], EX["do"][1] + k)
         attend_back(qkvb, attb, dob, c * 128, 1, (0, 1), 6, dk, dv, delta)
         grads_move(2)
         attend_back(qkvb, attb, dob, (1 - c) * 128, 1, (c,), 8, dk, dv, delta)
+        for d in xattb:
+            d.wait_send()
+        for k in (1, 2, 3):
+            from_heads_b("dqkv", qkvb, 0, k).start()
+        from_heads_b_own(qkvb, L0 + 6).start()
         grads_move(3)
+        attend_back(qkva, atta, doa, 128, 0, (0, 1), 2, dk, dv, delta)
+        grads_move(4)
+        attend_back(qkva, atta, doa, 256, 0, (0, 1), 4, dk, dv, delta)
 
     pl.run_scoped(back, pltpu.VMEM((N, 128), f32), pltpu.VMEM((N, 128), f32), pltpu.VMEM((8, N), f32))
+    xdq = from_heads_a("dqkv", qkva, qkv)
+    xdq.start()
+    ldq = from_heads_a_own("dqkv", qkva, qkv, L0 + 5)
+    ldq.start()
+    grads_move(5)
     xatt.wait_send()
-    for d in xattb:
-        d.wait_send()
-    send_do(done=True)
-    xb2 = [from_heads_b("dqkv", qkvb, 0, k) for k in (1, 2, 3)]
-    for d in xb2:
-        d.start()
-    lb2 = from_heads_b_own(qkvb, L0 + 6)
-    lb2.start()
+    for s in range(3):
+        for d in do_copies(s):
+            d.wait_send()
 
     gsend = cot
     for s in range(3):
         normed_rows(s)
 
-    def rows_back(s):
+    def rows_grad(s):
         r = pl.ds(s * T, T)
-        e_ = nt(qkv[0, r, :], wblock(R["wq"], slice(0, W)))
-        e_ += nt(qkv[1, r, :], wblock(R["wq"], slice(W, 2 * W)))
-        e_ += nt(qkv[2, r, :], wblock(R["wq"], slice(2 * W, 3 * W)))
+        v = nt(qkv[0, r, :], wblock(R["wq"], slice(0, W)))
+        v += nt(qkv[1, r, :], wblock(R["wq"], slice(W, 2 * W)))
+        return v + nt(qkv[2, r, :], wblock(R["wq"], slice(2 * W, 3 * W)))
+
+    def rows_back(s, e_):
+        r = pl.ds(s * T, T)
         n, inv = normalise(rows[s].astype(f32))
         gsend[s] = (mid[r, :] + norm_back(e_, n, inv, vec(V_NG))).astype(bf16)
         move_home(s, gsend.at[s], grh, S_GR, I_GR)
@@ -965,7 +1040,7 @@
             (V_VB, col_sum(qkv[2, r, :].astype(f32))),
         )
         for i, part in parts:
-            if s == 0:
+            if s == 2:
                 vg[i : i + 1, :] = part
             else:
                 vg[i : i + 1, :] += part
@@ -973,38 +1048,105 @@
     for m in range(3):
         move_out_done(m, R["cnth"].at[m], cnt, S_CNT, I_CNT)
         move_out_done(m, R["cotangent"].at[m], cot, S_COT, I_COT)
-    from_heads_a_own("dqkv", qkva, qkv, L0 + 5).wait()
-    wait_a("dqkv", qkv, False)
-    rows_back(0)
-    rows_back(1)
-    lb2.wait()
+    from_heads_b_own(qkvb, L0 + 6).wait()
     wait_b_tokens("dqkv", 3)
     for j in range(3):
         merge_b(qkv, j, j)
-    rows_back(2)
-    for j in range(3):
+    rows_back(2, rows_grad(2))
+    ldq.wait()
+    wait_a("dqkv", qkv, False)
+    vg[12:16, :] = jnp.zeros((4, W), f32)
+
+    def qkv_grad(j):
         w = tn(nbuf[...].reshape(3 * T, W), qkv[j]).astype(bf16)
         R["wq"][:, :, j * W : (j + 1) * W] = w.reshape(dps, KR, W)
+        if aligned:
+            rs1("Q%d" % j)
+
     if aligned:
-        rs1(Q_)
-        grads_move(4)
-        rs2(Q_)
-        grads_move(5)
-        rs3(Q_)
-        rs4(Q_)
-        y_send("Q", 2)
-        y_send("Q", 3)
-        y_final(Q_, outs[Q_])
-    else:
+        vx = R["vx"]
+        I_VEC = take(3)
+        I_VEZ = take(4)
+        pairs = (other, dp + dx, dp + dy)
+
+    def vec_copy(i):
+        return rcopy(vg, vx.at[i], I_VEC + i, I_VEC + i, (pairs[i], z))
+
+    def vec_add(i):
+        vec_copy(i).wait()
+        vg[...] += vx[i]
+
+    def vec_z(k):
+        return rcopy(vg, vx.at[2 + k], I_VEZ + k, I_VEZ + k, (dp, lax.rem(z + k, 4)))
+
+    def back_last(ebuf):
+        for s in range(2):
+            ebuf[s] = rows_grad(s)
+        qkv_grad(2)
+        qkv_grad(1)
+        if aligned:
+            rs2("Q2")
+        qkv_grad(0)
+        if aligned:
+            rs2("Q1")
+        rows_back(0, ebuf[0])
+        if aligned:
+            rs3("Q2")
+            rs2("Q0")
+        rows_back(1, ebuf[1])
+        if aligned:
+            vec_copy(0).start()
+            rs3("Q1")
+            rs4("Q2")
+            vec_add(0)
+            vec_copy(1).start()
+            rs3("Q0")
+            grads_move(6)
+            rs4("Q1")
+            y_send("Q2", 2)
+            vec_add(1)
+            vec_copy(2).start()
+            rs4("Q0")
+            y_send("Q1", 2)
+            y_send("Q2", 3)
+            vec_add(2)
+            for k in (1, 2, 3):
+                vec_z(k).start()
+            y_send("Q0", 2)
+            y_send("Q1", 3)
+            y_final("Q2")
+            y_send("Q0", 3)
+            y_final("Q1")
+            for k in (1, 2, 3):
+                recv(vx.at[2 + k], I_VEZ + k)
+            for k in (1, 2, 3):
+                vec_z(k).wait_send()
+            total = vg[...]
+            for k in (1, 2, 3):
+                total = total + vx[2 + k]
+            at = dp * 4 + z
+            n1, n2 = W // 32, F // 32
+            R["vs"][...] = pltpu.roll(total, lax.rem(W - at * n1, W), axis=1)[:, 0:128]
+            line = lax.broadcasted_iota(i32, (16, W), 0)
+            per_row = W // n2
+            ubr = jnp.sum(jnp.where(line == V_UB + lax.div(at, per_row), total, 0.0), axis=0, keepdims=True)
+            ubr = jnp.broadcast_to(ubr, (8, W))
+            R["vs"][8:16, :] = pltpu.roll(ubr, lax.rem(W - lax.rem(at, per_row) * n2, W), axis=1)[:, 0:128]
+            y_final("Q0")
+            for key in GC:
+                rs_done(key)
+
+    pl.run_scoped(back_last, pltpu.VMEM((2, T, W), f32))
+    if not aligned:
         save = [pltpu.make_async_copy(arrays[i], R[n], rs.at[L0 + 8 + i]) for i, n in enumerate(("gq", "go", "gu", "gd"))]
         for d in save:
             d.start()
         for d in save:
             d.wait()
-    vg[12:16, :] = jnp.zeros((4, W), f32)
-    from_heads_a("dqkv", qkva, qkv).wait_send()
-    for d in xb2:
-        d.wait_send()
+    xdq.wait_send()
+    for k in (1, 2, 3):
+        from_heads_b("dqkv", qkvb, 0, k).wait_send()
+    act_done()
     for s in range(3):
         move_home_done(s, gsend.at[s], grh, S_GR, I_GR)
     for m in range(3):
@@ -1013,9 +1155,20 @@
     assert count[0] <= cfg["sems"], count[0]
 
 
-def scatter_kernel(keep, grads, out):
+def finish_kernel(sizes, keep, grads, act_in, *refs):
+    n = 0 if sizes is None else 5
+    act_out, out = refs[n], refs[n + 1]
     places = lax.broadcasted_iota(i32, (out.shape[1], keep.shape[2]), 0)
     out[0] = nn((places == keep[0]).astype(f32).astype(bf16), grads[0])
+    act_out[...] = act_in[...]
+    if sizes is not None:
+
+        @pl.when(pl.program_id(0) == 0)
+        def _():
+            for i in range(4):
+                refs[n + 2 + i][...] = refs[i][...]
+            for i, width in enumerate(sizes):
+                refs[n + 6 + i][...] = refs[4][i : i + 1, 0:width]
 
 
 def body(patches, keep_index, shard_counts, cotangent, *shards):
@@ -1044,7 +1197,7 @@
         weights = tuple(lax.all_gather(w, axes, axis=0, tiled=True) for w in (wq, wo, wu, wd))
         weights = tuple(w.reshape(dps, -1, w.shape[1]) for w in weights)
         flat = None
-    cfg = dict(aligned=aligned, dps=dps, tokens=tokens, width=width, ff=ff, patch=patch, flat=flat, sems=260)
+    cfg = dict(aligned=aligned, dps=dps, tokens=tokens, width=width, ff=ff, patch=patch, flat=flat, sems=320)
     keep = keep_index
     ins = [
         ("patches", patches[:, 0], ANY),
@@ -1065,6 +1218,8 @@
             out.append(("g" + n, weights[i].shape, f32, VMEM))
         else:
             out.append(("g" + n, full[n], bf16, ANY))
+    if aligned:
+        out.append(("vs", (16, 128), f32, VMEM))
     t3 = 3 * tokens
     scratch = [("w" + n, full[n], bf16) for n in "qoud"]
     scratch += [
@@ -1094,6 +1249,7 @@
             ("zrr", (3, flat[4], 128), bf16),
             ("zrl", (3, flat[4], 128), bf16),
             ("vw", (dps, 64, 128), bf16),
+            ("vx", (6, 16, width), f32),
         ]
         scratch += [("rb1" + n, (4, *full[n][1:]), bf16) for n in "qoud"]
         scratch += [("rb2" + n, (3, *full[n][1:]), bf16) for n in "qoud"]
@@ -1110,22 +1266,35 @@
         cost_estimate=pl.CostEstimate(flops=flops, bytes_accessed=50_000_000, transcendentals=0),
         name="layer",
     )(*[a for _, a, _ in ins])
-    act, grh, vg, gq, go, gu, gd = results
-    patch_grad = pl.pallas_call(
-        scatter_kernel,
+    act, grh, vg, gq, go, gu, gd = results[:7]
+    whole = lambda v: pl.BlockSpec(v, lambda m: (0,) * len(v))
+    step = lambda *v: pl.BlockSpec((1, *v), lambda m: (m, 0, 0))
+    n = width // devices
+    sizes = [n] * 8 + [ff // devices] if aligned else None
+    extra = [gq, go, gu, gd, results[7]] if aligned else []
+    shapes = [(3, tokens, width, bf16), (3, patch, width, f32)]
+    specs = [step(tokens, width), step(patch, width)]
+    if aligned:
+        shapes += [(*v.shape, f32) for v in extra[:4]] + [(1, v, f32) for v in sizes]
+        specs += [whole(v.shape) for v in extra[:4]] + [whole((1, v)) for v in sizes]
+    done = pl.pallas_call(
+        functools.partial(finish_kernel, sizes),
         grid=(3,),
-        in_specs=[pl.BlockSpec((1, 1, tokens), lambda m: (m, 0, 0)), pl.BlockSpec((1, tokens, width), lambda m: (m, 0, 0))],
-        out_specs=pl.BlockSpec((1, patch, width), lambda m: (m, 0, 0)),
-        out_shape=jax.ShapeDtypeStruct((3, patch, width), f32),
+        in_specs=[step(1, tokens), step(tokens, width), step(tokens, width)] + [whole(v.shape) for v in extra],
+        out_specs=specs,
+        out_shape=[jax.ShapeDtypeStruct(v[:-1], v[-1]) for v in shapes],
         compiler_params=pltpu.CompilerParams(vmem_limit_bytes=32 * 1024 * 1024),
-        name="scatter",
-    )(keep, grh)
-    small = jnp.concatenate([vg[:8].reshape(8, devices, -1).transpose(1, 0, 2).reshape(devices, -1), vg[8 : 8 + ff // width].reshape(devices, -1)], axis=1)
-    small = lax.psum_scatter(small, ("dp", "blk"), scatter_dimension=0, tiled=True)[0]
-    n = width // devices
-    piece = [small[i * n : (i + 1) * n] for i in range(8)] + [small[8 * n :]]
-    if not aligned:
+        name="finish",
+    )(keep, grh, act, *extra)
+    act, patch_grad = done[:2]
+    if aligned:
+        gq, go, gu, gd = done[2:6]
+        piece = [v.reshape(-1) for v in done[6:]]
+    else:
         axes = ("dp", "blk")
+        small = [vg[:8].reshape(8, devices, n).transpose(1, 0, 2).reshape(devices, -1), vg[8 : 8 + ff // width].reshape(devices, -1)]
+        small = lax.psum_scatter(jnp.concatenate(small, axis=1), axes, scatter_dimension=0, tiled=True)[0]
+        piece = [small[i * n : (i + 1) * n] for i in range(8)] + [small[8 * n :]]
         gq, go, gu, gd = (
             lax.psum_scatter(w.reshape(-1, w.shape[-1]).astype(f32), axes, scatter_dimension=0, tiled=True) for w in (gq, go, gu, gd)
         )

time: 403 us -> 285 us (0.71)
  the two profiles are of different devices: /device:TPU:5 before, /device:TPU:0 now
where the time goes in v2:
time: 285 us; the launch traced here: 281 us
  Pallas kernels  270 us (95%)
  local copies, waits for them, and re-layouts  9.03 us (3%)
    pallas_call x1, Pallas kernels, body(): pl.pallas_call(functools.partial(layer_kernel, cfg, [n for n, _, _ in ins...  266 us
    unnamed x17, local copies, waits for them, and re-layouts  8.23 us

profile of v2, /device:TPU:0, one launch (start us, length us, event | category | flops | bytes accessed | tf_op | source)
XLA Modules:
  0.0 281.3 jit_solution(10279225961730117625)
XLA Ops:
  0.6 1.3 copy.36
  1.9 0.8 stack.35
  2.7 1.3 fusion.2.refs_8_
  4.0 0.0 copy-start.7
  4.0 266.4 %layer.1 = (bf16[3,256,768]{2,1,0:T(8,128)(2,1)}, bf16[3,256,768]{2,1,0:T(8,128)(2,1)}, f32[16,768]{1,0:T(8,128)}, f32[24,2304]{1,0:T(8,128)}, f32[24,768]{1,0:T...) custom-call(bf16[3,512,768]{2,1,0:T(8,128)(2,1)} %bitcast.40, s32[3,1,256]{2,1,0:T(1,128)} %keep.1, ...), custom_call_target="tpu_custom_call" | custom-call | flops 32614907904 | bytes 50000000 | tf_op jit(solution)/shard_map/layer/pallas_call | solution.py:1259
  270.4 0.0 copy-done.7
  270.4 0.0 copy-start
  270.4 1.3 copy-done
  271.6 0.0 copy-start.1
  271.6 1.3 copy-done.1
  272.9 0.0 copy-start.2
  272.9 1.0 copy-done.2
  273.9 0.0 copy-start.3
  273.9 1.0 copy-done.3
  274.8 0.0 copy-start.4
  274.8 0.9 copy-done.4
  275.8 0.0 copy-start.5
  275.8 0.9 copy-done.5
  276.6 0.0 copy-start.6
  276.7 0.7 copy-done.6
  277.3 3.7 %finish.1 = (bf16[3,256,768]{2,1,0:T(8,128)(2,1)}, f32[3,512,768]{2,1,0:T(8,128)}, f32[24,2304]{1,0:T(8,128)}, f32[24,768]{1,0:T(8,128)}, f32[24,3072]{1,0:T(8,1...) custom-call(s32[3,1,256]{2,1,0:T(1,128)S(1)} %copy-done.7, ...), custom_call_target="tpu_custom_call" | custom-call | tf_op jit(solution)/shard_map/finish/pallas_call | solution.py:1280
Async XLA Ops:
  4.0 266.4 %copy-start.7 = (s32[3,1,256]{2,1,0:T(1,128)S(1)}, s32[3,1,256]{2,1,0:T(1,128)}, u32[]{:S(2)}) copy-start(s32[3,1,256]{2,1,0:T(1,128)} %keep.1) | copy-start | bytes 9220
  270.4 1.3 copy-start
  271.6 1.3 copy-start.1
  272.9 1.0 copy-start.2
  273.9 1.0 copy-start.3
  274.8 0.9 copy-start.4
  275.8 0.9 copy-start.5
  276.6 0.7 copy-start.6

commit v3 on v2

--- a/solution.py
+++ b/solution.py
@@ -47,6 +47,14 @@
 
 def col_sum(v):
     return jnp.sum(v, axis=0, keepdims=True)
+
+
+def group_tile(t):
+    return t % 3 * 6 + t // 6 * 2 + t % 6 // 3
+
+
+def natural_tile(p):
+    return p % 6 // 2 * 6 + p % 2 * 3 + p // 6
 
 
 V_NG, V_NS, V_QB, V_VB, V_OB, V_MG, V_MS, V_DB, V_UB = range(9)
@@ -219,6 +227,9 @@
                 cols = slice(t * 128, (t + 1) * 128)
                 zbuf[slot, flat[a] + t * rows : flat[a] + (t + 1) * rows, :] = ref[:, cols]
 
+        def place(a, t):
+            return group_tile(t) if a == Q_ else t
+
         def unflatten(a, block):
             dst = gathered[a]
             if a == D_:
@@ -229,7 +240,8 @@
                 n, rows = dst.shape[-1] // 128, KR // 4
             for s in range(4):
                 for t in range(n):
-                    dst[block, s * rows : (s + 1) * rows, t * 128 : (t + 1) * 128] = zbuf[s, flat[a] + t * rows : flat[a] + (t + 1) * rows, :]
+                    p = place(a, t) * 128
+                    dst[block, s * rows : (s + 1) * rows, p : p + 128] = zbuf[s, flat[a] + t * rows : flat[a] + (t + 1) * rows, :]
 
         def ag_copies(a):
             ref = gathered[a]
@@ -403,7 +415,8 @@
                 total = zbuf[z, piece, :].astype(f32)
                 total = total + jnp.where(z >= 1, zrr[2, piece, :].astype(f32), 0.0)
                 total = total + jnp.where(z <= 2, zrl[2, piece, :].astype(f32), 0.0)
-                outs[a][:, t * 128 : (t + 1) * 128] = total
+                p = natural_tile(t) if a == Q_ else t
+                outs[a][:, p * 128 : (p + 1) * 128] = total
 
         def rs_done(key):
             for k in (1, 2, 3):
@@ -426,7 +439,7 @@
     qkv, qkva, qkvb = R["qkv"], R["qkva"], R["qkvb"]
     atta, attb, att, fromb = R["atta"], R["attb"], R["att"], R["fromb"]
     doa, dob, mid, vt, vg = R["doa"], R["dob"], R["mid"], R["vt"], R["vg"]
-    lse, grh, keep, act = R["lse"], R["grh"], R["keep"], R["act"]
+    lse, grh, keep, act, ysend = R["lse"], R["grh"], R["keep"], R["act"], R["ysend"]
     lane = lax.broadcasted_iota(i32, (1, 128), 1)
 
     if aligned:
@@ -457,8 +470,8 @@
             move_out(m, att.at[0, pl.ds(m * T, T)], rows, S_ROWS, I_ROWS)
             move_out(m, R["cnth"].at[m], cnt, S_CNT, I_CNT)
 
-    def send_cot():
-        for m in (2, 0, 1):
+    def send_cot(ms=(2, 0, 1)):
+        for m in ms:
             move_out(m, R["cotangent"].at[m], cot, S_COT, I_COT)
 
     if aligned:
@@ -471,6 +484,7 @@
             z_send(key, 3)
         z_wait("OU", 1)
         z_send("OU", 2)
+        z_send("D", 1)
         for key in "QV":
             z_wait(key, 3)
         unflatten(Q_, dp)
@@ -479,8 +493,12 @@
         ag1(4)
         z_wait("OU", 2)
         z_send("OU", 3)
+        z_wait("D", 1)
+        z_send("D", 2)
+        z_wait("OU", 3)
+        z_wait("D", 2)
+        z_send("D", 3)
         send_rows()
-        z_send("D", 1)
     else:
         full = [pltpu.make_async_copy(R[n], arrays[i], rs.at[L0 + 8 + i]) for i, n in enumerate(("sq", "so", "su", "sd"))]
         for d in full:
@@ -490,13 +508,14 @@
     if aligned:
         ag2(Q_)
         ag2(4)
-        z_wait("OU", 3)
         for a in (U_, O_):
             unflatten(a, dp)
-            ag1(a)
         ag3(Q_)
         ag3(4)
         ag4(4)
+        ag4(Q_)
+        for a in (U_, O_):
+            ag1(a)
         v = R["vw"][...].reshape(32 * 16, 128)
         to = lax.broadcasted_iota(i32, (128, W), 1)
         frm = lax.broadcasted_iota(i32, (128, W), 0)
@@ -525,25 +544,29 @@
         recv(rows.at[s], I_ROWS + s)
         recv(cnt.at[s], I_CNT + s)
         normed_rows(s)
-        if s == 2:
-            if aligned:
-                ag4(Q_)
-            else:
-                for d in full:
-                    d.wait()
+    if not aligned:
+        for d in full:
+            d.wait()
 
     def wblock(ref, cols=None):
         v = ref[...] if cols is None else ref[:, :, cols]
         return v.reshape(-1, v.shape[-1])
 
+    def group(t):
+        return wblock(R["wq"], slice(t * W, (t + 1) * W))
+
     def project(s):
-        for j in range(3):
-            v = nn(nbuf[s], wblock(R["wq"], slice(j * W, (j + 1) * W)))
-            if j == 0:
-                v = v + vec(V_QB)
-            if j == 2:
-                v = v + vec(V_VB)
-            qkv[j, pl.ds(mult(s * T, T), T), :] = v.astype(bf16)
+        r = pl.ds(mult(s * T, T), T)
+        for t in range(3):
+            v = nn(nbuf[s], group(t))
+            for j in range(3):
+                for k in range(2):
+                    at = k * HALF + t * 128
+                    x = v[:, (2 * j + k) * 128 : (2 * j + k + 1) * 128]
+                    if j != 1:
+                        row = V_QB if j == 0 else V_VB
+                        x = x + vt[row : row + 1, at : at + 128]
+                    qkv[j, r, at : at + 128] = x.astype(bf16)
 
     def dev_of(i):
         return (base + lax.rem(i, 2), 2 * h + lax.div(i, 2))
@@ -650,23 +673,20 @@
         if not aligned:
             return
         if step == 0:
-            z_wait("D", 1)
-            z_send("D", 2)
             for a in (U_, O_):
                 ag2(a)
         elif step == 1:
-            z_wait("D", 2)
-            z_send("D", 3)
-            send_cot()
-            for a in (U_, O_):
-                ag3(a)
+            send_cot((2,))
         elif step == 2:
             z_wait("D", 3)
             unflatten(D_, dp)
             ag1(D_)
         elif step == 3:
+            for a in (U_, O_):
+                ag3(a)
             ag2(D_)
         elif step == 4:
+            send_cot((0, 1))
             for a in (U_, O_):
                 ag4(a)
         elif step == 5:
@@ -730,16 +750,13 @@
                 o = jnp.where(lane // 64 == sel[0], outs[0], 0.0)
             dst[0, r, cols] = o.astype(bf16)
 
+    weights_ready(2)
     la.wait()
     wait_a("qkv", qkva, True)
 
-    for t in range(3):
+    for t in range(2):
         attend(qkva, atta, t * 128, 0, (0, 1), 2 * t)
         weights_ready(t)
-    xatt = from_heads_a("att", atta, att)
-    xatt.start()
-    latt = from_heads_a_own("att", atta, att, L0 + 2)
-    latt.start()
     lb.wait()
     wait_b_heads("qkv", qkvb)
     attend(qkvb, attb, c * 128, 1, (0, 1), 6)
@@ -750,6 +767,11 @@
         d.start()
     lattb = from_heads_b_own(attb, L0 + 3)
     lattb.start()
+    attend(qkva, atta, 256, 0, (0, 1), 4)
+    xatt = from_heads_a("att", atta, att)
+    xatt.start()
+    latt = from_heads_a_own("att", atta, att, L0 + 2)
+    latt.start()
     weights_ready(4)
     xa.wait_send()
     for d in xb:
@@ -780,26 +802,49 @@
         n, _ = normalise(v)
         nbuf[s] = (n * vec(V_MG) + vec(V_MS)).astype(bf16)
     weights_ready(6)
-    for s in (2, 0, 1):
-        recv(cot.at[s], I_COT + s)
-        o = live_of(s) * cot[s].astype(f32)
-        cot[s] = o.astype(bf16)
-        part = col_sum(o)
-        if s == 2:
-            vg[V_DB : V_DB + 1, :] = part
-        else:
-            vg[V_DB : V_DB + 1, :] += part
-
     FT = FR
 
-    def feed(res, gn2, n2t, tile):
+    ub = R["ub"]
+    outer = branch = cot
+
+    def hidden(s, up, j):
+        hid = nn(nbuf[s], up) + ub[pl.ds(j, 1), :]
+        phi_c = 0.5 * (1.0 + lax.erf(hid * 0.7071067811865476))
+        return hid, phi_c
+
+    def outer_rows():
+        for s in (2, 0, 1):
+            recv(cot.at[s], I_COT + s)
+            o = live_of(s) * cot[s].astype(f32)
+            cot[s] = o.astype(bf16)
+            part = col_sum(o)
+            if s == 2:
+                vg[V_DB : V_DB + 1, :] = part
+            else:
+                vg[V_DB : V_DB + 1, :] += part
+
+    def feed(acc, n2t, tile):
         act_s, gh_s = tile.at[0], tile.at[1]
         for s in range(3):
             n2t[:, s * T : (s + 1) * T] = nbuf[s].T
-        res[...] = jnp.zeros_like(res)
-        gn2[...] = jnp.zeros_like(gn2)
-        outer = branch = cot
-        ub = R["ub"]
+            acc[s * T : (s + 1) * T, :] = mid[s * T : (s + 1) * T, :] + vec(V_DB)
+
+        @pl.loop(0, dps)
+        def _(j):
+            up = wblock(R["wu"], ds128(j * FT, FT))
+            down = R["wd"][j]
+
+            @pl.loop(0, 3)
+            def _(s):
+                hid, phi_c = hidden(s, up, j)
+                acc[slot_rows(s), :] += nn((hid * phi_c).astype(bf16), down)
+
+        for s in (2, 0, 1):
+            r = pl.ds(s * T, T)
+            ysend[s] = (live_of(s) * acc[r, :]).astype(bf16)
+            move_home(s, ysend.at[s], act, S_ACT, I_ACT)
+            acc[r, :] = jnp.zeros((T, W), f32)
+        outer_rows()
 
         def tile_pair(i):
             @pl.loop(2 * i, 2 * i + 2)
@@ -810,20 +855,16 @@
             cols = ds128(j * FT, FT)
             up = wblock(R["wu"], cols)
             down = R["wd"][j]
-            ub_j = ub[pl.ds(j, 1), :]
 
             @pl.loop(0, 3, init_carry=jnp.zeros((1, FT), f32))
             def bias_part(s, carry):
                 r = slot_rows(s)
-                hid = nn(nbuf[s], up) + ub_j
-                phi_c = 0.5 * (1.0 + lax.erf(hid * 0.7071067811865476))
-                act_low = (hid * phi_c).astype(bf16)
-                act_s[r, :] = act_low
-                res[r, :] += nn(act_low, down)
+                hid, phi_c = hidden(s, up, j)
+                act_s[r, :] = (hid * phi_c).astype(bf16)
                 slope = phi_c + hid * jnp.exp2(hid * hid * (-0.5 * LOG2E)) * 0.3989422804014327
                 gh = (nt(outer[s], down) * slope).astype(bf16)
                 gh_s[r, :] = gh
-                gn2[r, :] += nt(gh, up)
+                acc[r, :] += nt(gh, up)
                 return carry + col_sum(gh.astype(f32))
 
             ub[pl.ds(j, 1), :] = bias_part
@@ -840,14 +881,13 @@
                     rs2_pair("D", i - 1)
                 if i == 2:
                     rs2("U0")
+                if i == 3:
+                    rs3("U0")
 
         for s in (2, 0, 1):
             r = pl.ds(s * T, T)
-            v = mid[r, :]
-            y = live_of(s) * (v + res[r, :] + vec(V_DB))
-            n2t[r, :] = y.astype(bf16)
-            n, inv = normalise(v)
-            e_ = gn2[r, :]
+            n, inv = normalise(mid[r, :])
+            e_ = acc[r, :]
             gm = outer[s].astype(f32) + norm_back(e_, n, inv, vec(V_MG))
             mid[r, :] = gm
             low = gm.astype(bf16)
@@ -862,14 +902,11 @@
         for q in range(2):
             piece = tn(att[0, :, q * HALF : (q + 1) * HALF], branch[...].reshape(3 * T, W)).astype(bf16)
             R["wo"][q * (dps // 2) : (q + 1) * (dps // 2)] = piece.reshape(dps // 2, KR, W)
-        att[0] = n2t[...]
-        for s in (2, 0, 1):
-            move_home(s, att.at[0, pl.ds(s * T, T)], act, S_ACT, I_ACT)
         grads_move(0)
 
     def act_done():
         for s in range(3):
-            move_home_done(s, att.at[0, pl.ds(s * T, T)], act, S_ACT, I_ACT)
+            move_home_done(s, ysend.at[s], act, S_ACT, I_ACT)
 
     do3 = R["nbuf"]
 
@@ -894,34 +931,32 @@
         if step == 0:
             rs1("O")
             rs2_pair("D", 3)
-            rs3("U0")
             rs2("U1")
+        elif step == 1:
+            rs4("U0")
+            rs2("O")
+        elif step == 2:
             rs3("D")
-        elif step == 1:
-            rs2("O")
-            rs4("U0")
             rs3("U1")
-        elif step == 2:
-            rs4("D")
-            rs3("O")
             y_send("U0", 2)
         elif step == 3:
+            rs3("O")
+        elif step == 4:
+            rs4("D")
             rs4("U1")
+            rs4("O")
+            y_send("U0", 3)
+        elif step == 5:
             y_send("D", 2)
-            y_send("U0", 3)
-        elif step == 4:
-            rs4("O")
+            y_send("U1", 2)
+            y_send("O", 2)
+        elif step == 6:
             y_send("D", 3)
-            y_send("U1", 2)
-            y_final("U0")
-        elif step == 5:
-            y_send("O", 2)
             y_send("U1", 3)
-            y_final("D")
-        elif step == 6:
             y_send("O", 3)
-            y_final("U1")
-            y_final("O")
+        elif step == 8:
+            for key in ("U0", "D", "U1", "O"):
+                y_final(key)
 
     per = W // FT
     for q in range(dps):
@@ -929,7 +964,6 @@
     pl.run_scoped(
         feed,
         pltpu.VMEM((3 * T, W), f32),
-        pltpu.VMEM((3 * T, W), f32),
         pltpu.VMEM((W, 3 * T), bf16),
         pltpu.VMEM((2, 3 * T, FT), bf16),
     )
@@ -939,8 +973,6 @@
     for j in range(2):
         doa[ds128(2 * T * c + j * T, T), :] = do3[j, :, ds128(HALF * c, HALF)]
     dob[ds128(T * g, T), :] = do3[2, :, ds128(HALF * e + 128 * c, 256)]
-    recv(doa.at[ds128(2 * T * (1 - c), T)], EX["do"][0])
-    recv(doa.at[ds128(2 * T * (1 - c) + T, T)], L0 + 4)
 
     def attend_back(src, o_ref, d_ref, col, bi, sel, lrow, dk, dv, delta):
         cols = ds128(col, 128)
@@ -989,44 +1021,37 @@
         src[1, :, cols] = (dk[...] * 0.125).astype(bf16)
         src[2, :, cols] = dv[...].astype(bf16)
 
-    def back(dk, dv, delta):
-        attend_back(qkva, atta, doa, 0, 0, (0, 1), 0, dk, dv, delta)
-        grads_move(1)
-        for k in (1, 2, 3):
-            recv(dob.at[ds128(T * lax.rem(g + 4 - k, 4), T)], EX["do"][1] + k)
-        attend_back(qkvb, attb, dob, c * 128, 1, (0, 1), 6, dk, dv, delta)
-        grads_move(2)
-        attend_back(qkvb, attb, dob, (1 - c) * 128, 1, (c,), 8, dk, dv, delta)
-        for d in xattb:
-            d.wait_send()
-        for k in (1, 2, 3):
-            from_heads_b("dqkv", qkvb, 0, k).start()
-        from_heads_b_own(qkvb, L0 + 6).start()
-        grads_move(3)
-        attend_back(qkva, atta, doa, 128, 0, (0, 1), 2, dk, dv, delta)
-        grads_move(4)
-        attend_back(qkva, atta, doa, 256, 0, (0, 1), 4, dk, dv, delta)
-
-    pl.run_scoped(back, pltpu.VMEM((N, 128), f32), pltpu.VMEM((N, 128), f32), pltpu.VMEM((8, N), f32))
-    xdq = from_heads_a("dqkv", qkva, qkv)
-    xdq.start()
-    ldq = from_heads_a_own("dqkv", qkva, qkv, L0 + 5)
-    ldq.start()
-    grads_move(5)
-    xatt.wait_send()
-    for s in range(3):
-        for d in do_copies(s):
-            d.wait_send()
+    I_DQA = take(6)
+
+    def dq_copy(t):
+        sref = qkva.at[:, ds128(2 * T * (1 - c), 2 * T), pl.ds(t * 128, 128)]
+        dref = qkv.at[:, pl.ds(0, 2 * T), ds128(HALF * c + t * 128, 128)]
+        return rcopy(sref, dref, I_DQA + t, I_DQA + t, (other, z))
+
+    def dq_own(t):
+        sref = qkva.at[:, ds128(2 * T * c, 2 * T), pl.ds(t * 128, 128)]
+        dref = qkv.at[:, pl.ds(0, 2 * T), ds128(HALF * c + t * 128, 128)]
+        return pltpu.make_async_copy(sref, dref, rs.at[I_DQA + 3 + t])
+
+    def strips(t, r):
+        return jnp.concatenate([qkv[j, r, k * HALF + t * 128 : k * HALF + (t + 1) * 128] for j in range(3) for k in range(2)], axis=1)
 
     gsend = cot
-    for s in range(3):
-        normed_rows(s)
-
-    def rows_grad(s):
-        r = pl.ds(s * T, T)
-        v = nt(qkv[0, r, :], wblock(R["wq"], slice(0, W)))
-        v += nt(qkv[1, r, :], wblock(R["wq"], slice(W, 2 * W)))
-        return v + nt(qkv[2, r, :], wblock(R["wq"], slice(2 * W, 3 * W)))
+    if aligned:
+        vx = R["vx"]
+        I_VEC = take(3)
+        I_VEZ = take(4)
+        pairs = (other, dp + dx, dp + dy)
+
+    def vec_copy(i):
+        return rcopy(vg, vx.at[i], I_VEC + i, I_VEC + i, (pairs[i], z))
+
+    def vec_add(i):
+        vec_copy(i).wait()
+        vg[...] += vx[i]
+
+    def vec_z(k):
+        return rcopy(vg, vx.at[2 + k], I_VEZ + k, I_VEZ + k, (dp, lax.rem(z + k, 4)))
 
     def rows_back(s, e_):
         r = pl.ds(s * T, T)
@@ -1045,77 +1070,96 @@
             else:
                 vg[i : i + 1, :] += part
 
-    for m in range(3):
-        move_out_done(m, R["cnth"].at[m], cnt, S_CNT, I_CNT)
-        move_out_done(m, R["cotangent"].at[m], cot, S_COT, I_COT)
-    from_heads_b_own(qkvb, L0 + 6).wait()
-    wait_b_tokens("dqkv", 3)
-    for j in range(3):
-        merge_b(qkv, j, j)
-    rows_back(2, rows_grad(2))
-    ldq.wait()
-    wait_a("dqkv", qkv, False)
-    vg[12:16, :] = jnp.zeros((4, W), f32)
-
-    def qkv_grad(j):
-        w = tn(nbuf[...].reshape(3 * T, W), qkv[j]).astype(bf16)
-        R["wq"][:, :, j * W : (j + 1) * W] = w.reshape(dps, KR, W)
+    def close_group(t, ebuf):
+        dq_own(t).wait()
+        recv(qkv.at[:, pl.ds(0, 2 * T), ds128(HALF * (1 - c) + t * 128, 128)], I_DQA + t)
+        for s in range(2):
+            part = nt(strips(t, pl.ds(s * T, T)), group(t))
+            if t == 0:
+                ebuf[s] = part
+            else:
+                ebuf[s] += part
+        w = tn(nbuf[...].reshape(3 * T, W), strips(t, pl.ds(0, 3 * T))).astype(bf16)
+        R["wq"][:, :, t * W : (t + 1) * W] = w.reshape(dps, KR, W)
         if aligned:
-            rs1("Q%d" % j)
-
-    if aligned:
-        vx = R["vx"]
-        I_VEC = take(3)
-        I_VEZ = take(4)
-        pairs = (other, dp + dx, dp + dy)
-
-    def vec_copy(i):
-        return rcopy(vg, vx.at[i], I_VEC + i, I_VEC + i, (pairs[i], z))
-
-    def vec_add(i):
-        vec_copy(i).wait()
-        vg[...] += vx[i]
-
-    def vec_z(k):
-        return rcopy(vg, vx.at[2 + k], I_VEZ + k, I_VEZ + k, (dp, lax.rem(z + k, 4)))
-
-    def back_last(ebuf):
-        for s in range(2):
-            ebuf[s] = rows_grad(s)
-        qkv_grad(2)
-        qkv_grad(1)
+            rs1("Q%d" % t)
+
+    def back(dk, dv, delta, ebuf):
+        for k in (1, 2, 3):
+            recv(dob.at[ds128(T * lax.rem(g + 4 - k, 4), T)], EX["do"][1] + k)
+        attend_back(qkvb, attb, dob, c * 128, 1, (0, 1), 6, dk, dv, delta)
+        grads_move(1)
+        attend_back(qkvb, attb, dob, (1 - c) * 128, 1, (c,), 8, dk, dv, delta)
+        for d in xattb:
+            d.wait_send()
+        for k in (1, 2, 3):
+            from_heads_b("dqkv", qkvb, 0, k).start()
+        from_heads_b_own(qkvb, L0 + 6).start()
+        grads_move(2)
+        recv(doa.at[ds128(2 * T * (1 - c), T)], EX["do"][0])
+        recv(doa.at[ds128(2 * T * (1 - c) + T, T)], L0 + 4)
+        attend_back(qkva, atta, doa, 0, 0, (0, 1), 0, dk, dv, delta)
+        dq_copy(0).start()
+        dq_own(0).start()
+        grads_move(3)
+        for s in range(3):
+            for d in do_copies(s):
+                d.wait_send()
+        for s in range(3):
+            normed_rows(s)
+        for m in range(3):
+            move_out_done(m, R["cnth"].at[m], cnt, S_CNT, I_CNT)
+            move_out_done(m, R["cotangent"].at[m], cot, S_COT, I_COT)
+        attend_back(qkva, atta, doa, 128, 0, (0, 1), 2, dk, dv, delta)
+        dq_copy(1).start()
+        dq_own(1).start()
+        grads_move(4)
+        from_heads_b_own(qkvb, L0 + 6).wait()
+        wait_b_tokens("dqkv", 3)
+        for j in range(3):
+            merge_b(qkv, j, j)
+        r = pl.ds(2 * T, T)
+        e_ = nt(strips(0, r), group(0)) + nt(strips(1, r), group(1)) + nt(strips(2, r), group(2))
+        rows_back(2, e_)
+        close_group(0, ebuf)
+        grads_move(5)
+        attend_back(qkva, atta, doa, 256, 0, (0, 1), 4, dk, dv, delta)
+        dq_copy(2).start()
+        dq_own(2).start()
+        close_group(1, ebuf)
         if aligned:
-            rs2("Q2")
-        qkv_grad(0)
-        if aligned:
-            rs2("Q1")
+            rs2("Q0")
+        close_group(2, ebuf)
+        grads_move(6)
         rows_back(0, ebuf[0])
         if aligned:
-            rs3("Q2")
-            rs2("Q0")
+            rs3("Q0")
+            rs2("Q1")
         rows_back(1, ebuf[1])
+        vg[12:16, :] = jnp.zeros((4, W), f32)
         if aligned:
             vec_copy(0).start()
+            rs2("Q2")
+            rs4("Q0")
             rs3("Q1")
-            rs4("Q2")
             vec_add(0)
             vec_copy(1).start()
-            rs3("Q0")
-            grads_move(6)
+            rs3("Q2")
             rs4("Q1")
-            y_send("Q2", 2)
+            y_send("Q0", 2)
             vec_add(1)
             vec_copy(2).start()
-            rs4("Q0")
+            rs4("Q2")
             y_send("Q1", 2)
-            y_send("Q2", 3)
+            y_send("Q0", 3)
             vec_add(2)
             for k in (1, 2, 3):
                 vec_z(k).start()
-            y_send("Q0", 2)
+            grads_move(8)
+            y_send("Q2", 2)
             y_send("Q1", 3)
-            y_final("Q2")
-            y_send("Q0", 3)
+            y_final("Q0")
+            y_send("Q2", 3)
             y_final("Q1")
             for k in (1, 2, 3):
                 recv(vx.at[2 + k], I_VEZ + k)
@@ -1132,18 +1176,20 @@
             ubr = jnp.sum(jnp.where(line == V_UB + lax.div(at, per_row), total, 0.0), axis=0, keepdims=True)
             ubr = jnp.broadcast_to(ubr, (8, W))
             R["vs"][8:16, :] = pltpu.roll(ubr, lax.rem(W - lax.rem(at, per_row) * n2, W), axis=1)[:, 0:128]
-            y_final("Q0")
+            y_final("Q2")
             for key in GC:
                 rs_done(key)
 
-    pl.run_scoped(back_last, pltpu.VMEM((2, T, W), f32))
+    pl.run_scoped(back, pltpu.VMEM((N, 128), f32), pltpu.VMEM((N, 128), f32), pltpu.VMEM((8, N), f32), pltpu.VMEM((2, T, W), f32))
+    xatt.wait_send()
     if not aligned:
         save = [pltpu.make_async_copy(arrays[i], R[n], rs.at[L0 + 8 + i]) for i, n in enumerate(("gq", "go", "gu", "gd"))]
         for d in save:
             d.start()
         for d in save:
             d.wait()
-    xdq.wait_send()
+    for t in range(3):
+        dq_copy(t).wait_send()
     for k in (1, 2, 3):
         from_heads_b("dqkv", qkvb, 0, k).wait_send()
     act_done()
@@ -1196,6 +1242,8 @@
         table = jnp.concatenate([table, table_ub, jnp.zeros((16 - 8 - ff // width, width), f32)])
         weights = tuple(lax.all_gather(w, axes, axis=0, tiled=True) for w in (wq, wo, wu, wd))
         weights = tuple(w.reshape(dps, -1, w.shape[1]) for w in weights)
+        held = weights[0].reshape(dps, kr, 3, 2, 3, width // 6).transpose(0, 1, 4, 2, 3, 5).reshape(dps, kr, 3 * width)
+        weights = (held, *weights[1:])
         flat = None
     cfg = dict(aligned=aligned, dps=dps, tokens=tokens, width=width, ff=ff, patch=patch, flat=flat, sems=320)
     keep = keep_index
@@ -1238,6 +1286,7 @@
         ("doa", (4 * tokens, width // 2), bf16),
         ("dob", (4 * tokens, 256), bf16),
         ("mid", (t3, width), f32),
+        ("ysend", (3, tokens, width), bf16),
         ("vt", (16, width), f32),
         ("lse", (16, 4 * tokens), f32),
         ("bias", (2, 4 * tokens, 128), bf16),
@@ -1295,6 +1344,7 @@
         small = [vg[:8].reshape(8, devices, n).transpose(1, 0, 2).reshape(devices, -1), vg[8 : 8 + ff // width].reshape(devices, -1)]
         small = lax.psum_scatter(jnp.concatenate(small, axis=1), axes, scatter_dimension=0, tiled=True)[0]
         piece = [small[i * n : (i + 1) * n] for i in range(8)] + [small[8 * n :]]
+        gq = gq.reshape(dps, kr, 3, 3, 2, width // 6).transpose(0, 1, 3, 4, 2, 5).reshape(dps, kr, 3 * width)
         gq, go, gu, gd = (
             lax.psum_scatter(w.reshape(-1, w.shape[-1]).astype(f32), axes, scatter_dimension=0, tiled=True) for w in (gq, go, gu, gd)
         )

time: 285 us -> 272 us (0.954)
  the two profiles are of different devices: /device:TPU:0 before, /device:TPU:5 now
where the time goes in v3:
time: 272 us; the launch traced here: 268 us
  Pallas kernels  257 us (94%)
  local copies, waits for them, and re-layouts  9.03 us (3%)
    pallas_call x1, Pallas kernels, body(): pl.pallas_call(functools.partial(layer_kernel, cfg, [n for n, _, _ in ins...  253 us
    unnamed x17, local copies, waits for them, and re-layouts  8.23 us

profile of v3, /device:TPU:5, one launch (start us, length us, event | category | flops | bytes accessed | tf_op | source)
XLA Modules:
  0.0 268.1 jit_solution(5192217835205702791)
XLA Ops:
  0.6 1.3 copy.36
  1.9 0.8 stack.35
  2.7 1.3 fusion.2.refs_8_
  4.0 0.0 copy-start.7
  4.0 253.2 %layer.1 = (bf16[3,256,768]{2,1,0:T(8,128)(2,1)}, bf16[3,256,768]{2,1,0:T(8,128)(2,1)}, f32[16,768]{1,0:T(8,128)}, f32[24,2304]{1,0:T(8,128)}, f32[24,768]{1,0:T...) custom-call(bf16[3,512,768]{2,1,0:T(8,128)(2,1)} %bitcast.40, s32[3,1,256]{2,1,0:T(1,128)} %keep.1, ...), custom_call_target="tpu_custom_call" | custom-call | flops 32614907904 | bytes 50000000 | tf_op jit(solution)/shard_map/layer/pallas_call | solution.py:1308
  257.2 0.0 copy-done.7
  257.2 0.0 copy-start
  257.2 1.3 copy-done
  258.5 0.0 copy-start.1
  258.5 1.3 copy-done.1
  259.7 0.0 copy-start.2
  259.7 1.0 copy-done.2
  260.7 0.0 copy-start.3
  260.7 1.0 copy-done.3
  261.6 0.0 copy-start.4
  261.6 0.9 copy-done.4
  262.6 0.0 copy-start.5
  262.6 0.9 copy-done.5
  263.5 0.0 copy-start.6
  263.5 0.7 copy-done.6
  264.2 3.7 %finish.1 = (bf16[3,256,768]{2,1,0:T(8,128)(2,1)}, f32[3,512,768]{2,1,0:T(8,128)}, f32[24,2304]{1,0:T(8,128)}, f32[24,768]{1,0:T(8,128)}, f32[24,3072]{1,0:T(8,1...) custom-call(s32[3,1,256]{2,1,0:T(1,128)S(1)} %copy-done.7, ...), custom_call_target="tpu_custom_call" | custom-call | tf_op jit(solution)/shard_map/finish/pallas_call | solution.py:1329
Async XLA Ops:
  4.0 253.2 %copy-start.7 = (s32[3,1,256]{2,1,0:T(1,128)S(1)}, s32[3,1,256]{2,1,0:T(1,128)}, u32[]{:S(2)}) copy-start(s32[3,1,256]{2,1,0:T(1,128)} %keep.1) | copy-start | bytes 9220
  257.2 1.3 copy-start
  258.5 1.3 copy-start.1
  259.7 1.0 copy-start.2
  260.7 1.0 copy-start.3
  261.6 0.9 copy-start.4
  262.6 0.9 copy-start.5
  263.5 0.7 copy-start.6

commit v4 on v3

--- a/solution.py
+++ b/solution.py
@@ -447,7 +447,7 @@
             flatten(a, R[name], z)
     for m in range(3):
         for b in range(4):
-            R["cnth"][m, b : b + 1, :] = jnp.full((1, 128), R["counts"][m, b], i32).astype(f32).astype(bf16)
+            R["cnth"][m, b : b + 1, :] = jnp.full((1, 128), R["counts"][m, 0, b], i32).astype(f32).astype(bf16)
         R["cnth"][m, 4:, :] = jnp.zeros((12, 128), bf16)
 
     def pick_rows(pbuf, psem):
@@ -932,31 +932,34 @@
             rs1("O")
             rs2_pair("D", 3)
             rs2("U1")
+            rs4("U0")
         elif step == 1:
-            rs4("U0")
+            y_send("U0", 2)
+        elif step == 2:
             rs2("O")
-        elif step == 2:
             rs3("D")
+        elif step == 3:
             rs3("U1")
-            y_send("U0", 2)
-        elif step == 3:
             rs3("O")
         elif step == 4:
+            y_send("U0", 3)
             rs4("D")
             rs4("U1")
             rs4("O")
-            y_send("U0", 3)
         elif step == 5:
             y_send("D", 2)
             y_send("U1", 2)
             y_send("O", 2)
         elif step == 6:
+            y_send("U1", 3)
+            y_final("U0")
+        elif step == 7:
             y_send("D", 3)
-            y_send("U1", 3)
             y_send("O", 3)
+            y_final("U1")
         elif step == 8:
-            for key in ("U0", "D", "U1", "O"):
-                y_final(key)
+            y_final("D")
+            y_final("O")
 
     per = W // FT
     for q in range(dps):
@@ -1142,6 +1145,7 @@
             rs2("Q2")
             rs4("Q0")
             rs3("Q1")
+            grads_move(7)
             vec_add(0)
             vec_copy(1).start()
             rs3("Q2")
@@ -1250,7 +1254,7 @@
     ins = [
         ("patches", patches[:, 0], ANY),
         ("keep", keep, VMEM),
-        ("counts", shard_counts[:, 0], SMEM),
+        ("counts", shard_counts, SMEM),
         ("cotangent", cotangent[:, 0], ANY),
     ]
     ins += [(n, w, VMEM if aligned else ANY) for n, w in zip(("sq", "so", "su", "sd"), weights)]
@@ -1332,7 +1336,7 @@
         in_specs=[step(1, tokens), step(tokens, width), step(tokens, width)] + [whole(v.shape) for v in extra],
         out_specs=specs,
         out_shape=[jax.ShapeDtypeStruct(v[:-1], v[-1]) for v in shapes],
-        compiler_params=pltpu.CompilerParams(vmem_limit_bytes=32 * 1024 * 1024),
+        compiler_params=pltpu.CompilerParams(vmem_limit_bytes=64 * 1024 * 1024 - 512 * 1024),
         name="finish",
     )(keep, grh, act, *extra)
     act, patch_grad = done[:2]

time: 272 us -> 264 us (0.971)
  local copies, waits for them, and re-layouts: 9.03 us -> 0.8 us
    unnamed x17 -> x0, local copies, waits for them, and re-layouts: 8.23 us -> none
where the time goes in v4:
time: 264 us; the launch traced here: 261 us
  Pallas kernels  258 us (98%)
    pallas_call x1, Pallas kernels, body(): pl.pallas_call(functools.partial(layer_kernel, cfg, [n for n, _, _ in ins...  252 us
    pallas_call x1, Pallas kernels, body(): pl.pallas_call(functools.partial(finish_kernel, sizes), grid=(3,), in_spe...  5.87 us

profile of v4, /device:TPU:5, one launch (start us, length us, event | category | flops | bytes accessed | tf_op | source)
XLA Modules:
  0.0 261.0 jit_solution(12413221834951049664)
XLA Ops:
  0.6 0.8 stack.35
  1.4 1.3 fusion.2.refs_8_
  2.7 252.1 %layer.1 = (bf16[3,256,768]{2,1,0:T(8,128)(2,1)}, bf16[3,256,768]{2,1,0:T(8,128)(2,1)}, f32[16,768]{1,0:T(8,128)}, f32[24,2304]{1,0:T(8,128)}, f32[24,768]{1,0:T...) custom-call(bf16[3,512,768]{2,1,0:T(8,128)(2,1)} %bitcast.36, s32[3,1,256]{2,1,0:T(1,128)} %keep.1, ...), custom_call_target="tpu_custom_call" | custom-call | flops 32614907904 | bytes 50000000 | tf_op jit(solution)/shard_map/layer/pallas_call | solution.py:1312
  254.8 5.9 %finish.1 = (bf16[3,256,768]{2,1,0:T(8,128)(2,1)}, f32[3,512,768]{2,1,0:T(8,128)}, f32[24,2304]{1,0:T(8,128)}, f32[24,768]{1,0:T(8,128)}, f32[24,3072]{1,0:T(8,1...) custom-call(s32[3,1,256]{2,1,0:T(1,128)} %keep.1, ...), custom_call_target="tpu_custom_call" | custom-call | tf_op jit(solution)/shard_map/finish/pallas_call | solution.py:1333

commit v5 on v4

--- a/solution.py
+++ b/solution.py
@@ -458,6 +458,7 @@
         if aligned:
             z_send("Q", 1)
             z_send("V", 1)
+            z_send("OU", 1)
         for m in range(3):
             copies[m].wait()
             spread = (lax.broadcasted_iota(i32, (cfg["patch"], T), 0) == keep[m]).astype(f32).astype(bf16)
@@ -475,16 +476,15 @@
             move_out(m, R["cotangent"].at[m], cot, S_COT, I_COT)
 
     if aligned:
+        z_wait("OU", 1)
         for key in "QV":
             z_wait(key, 1)
             z_send(key, 2)
-        z_send("OU", 1)
+        z_send("D", 1)
         for key in "QV":
             z_wait(key, 2)
             z_send(key, 3)
-        z_wait("OU", 1)
         z_send("OU", 2)
-        z_send("D", 1)
         for key in "QV":
             z_wait(key, 3)
         unflatten(Q_, dp)
@@ -492,13 +492,12 @@
         unflatten(4, dp)
         ag1(4)
         z_wait("OU", 2)
+        z_wait("D", 1)
         z_send("OU", 3)
-        z_wait("D", 1)
         z_send("D", 2)
+        z_wait("D", 2)
         z_wait("OU", 3)
-        z_wait("D", 2)
         z_send("D", 3)
-        send_rows()
     else:
         full = [pltpu.make_async_copy(R[n], arrays[i], rs.at[L0 + 8 + i]) for i, n in enumerate(("sq", "so", "su", "sd"))]
         for d in full:
@@ -508,14 +507,15 @@
     if aligned:
         ag2(Q_)
         ag2(4)
-        for a in (U_, O_):
-            unflatten(a, dp)
+        send_rows()
+        unflatten(O_, dp)
+        ag1(O_)
         ag3(Q_)
         ag3(4)
+        unflatten(U_, dp)
         ag4(4)
         ag4(Q_)
-        for a in (U_, O_):
-            ag1(a)
+        ag1(U_)
         v = R["vw"][...].reshape(32 * 16, 128)
         to = lax.broadcasted_iota(i32, (128, W), 1)
         frm = lax.broadcasted_iota(i32, (128, W), 0)
@@ -675,21 +675,20 @@
         if step == 0:
             for a in (U_, O_):
                 ag2(a)
-        elif step == 1:
             send_cot((2,))
         elif step == 2:
             z_wait("D", 3)
             unflatten(D_, dp)
             ag1(D_)
         elif step == 3:
+            ag2(D_)
+        elif step == 4:
             for a in (U_, O_):
                 ag3(a)
-            ag2(D_)
-        elif step == 4:
+        elif step == 5:
             send_cot((0, 1))
             for a in (U_, O_):
                 ag4(a)
-        elif step == 5:
             ag3(D_)
         elif step == 6:
             ag4(D_)
@@ -756,7 +755,8 @@
 
     for t in range(2):
         attend(qkva, atta, t * 128, 0, (0, 1), 2 * t)
-        weights_ready(t)
+        if t == 0:
+            weights_ready(0)
     lb.wait()
     wait_b_heads("qkv", qkvb)
     attend(qkvb, attb, c * 128, 1, (0, 1), 6)
@@ -767,12 +767,13 @@
         d.start()
     lattb = from_heads_b_own(attb, L0 + 3)
     lattb.start()
+    weights_ready(4)
     attend(qkva, atta, 256, 0, (0, 1), 4)
     xatt = from_heads_a("att", atta, att)
     xatt.start()
     latt = from_heads_a_own("att", atta, att, L0 + 2)
     latt.start()
-    weights_ready(4)
+    weights_ready(5)
     xa.wait_send()
     for d in xb:
         d.wait_send()
@@ -795,7 +796,6 @@
             lattb.wait()
             wait_b_tokens("att", 1)
             merge_b(att, 0, 0)
-            weights_ready(5)
         r = pl.ds(s * T, T)
         v = nn(att[0, r, :], wblock(R["wo"])) + vec(V_OB) + rows[s].astype(f32)
         mid[r, :] = v
@@ -932,21 +932,21 @@
             rs1("O")
             rs2_pair("D", 3)
             rs2("U1")
+        elif step == 1:
+            rs2("O")
             rs4("U0")
-        elif step == 1:
-            y_send("U0", 2)
         elif step == 2:
-            rs2("O")
             rs3("D")
         elif step == 3:
+            y_send("U0", 2)
             rs3("U1")
             rs3("O")
         elif step == 4:
-            y_send("U0", 3)
             rs4("D")
             rs4("U1")
             rs4("O")
         elif step == 5:
+            y_send("U0", 3)
             y_send("D", 2)
             y_send("U1", 2)
             y_send("O", 2)

time: 264 us -> 262 us (level)
  the two profiles are of different devices: /device:TPU:5 before, /device:TPU:11 now
where the time goes in v5:
time: 262 us; the launch traced here: 258 us
  Pallas kernels  255 us (97%)
    pallas_call x1, Pallas kernels, body(): pl.pallas_call(functools.partial(layer_kernel, cfg, [n for n, _, _ in ins...  250 us
    pallas_call x1, Pallas kernels, body(): pl.pallas_call(functools.partial(finish_kernel, sizes), grid=(3,), in_spe...  5.87 us

profile of v5, /device:TPU:11, one launch (start us, length us, event | category | flops | bytes accessed | tf_op | source)
XLA Modules:
  0.0 258.3 jit_solution(8969979438821463588)
XLA Ops:
  0.6 0.8 stack.35
  1.4 1.3 fusion.2.refs_8_
  2.7 249.5 %layer.1 = (bf16[3,256,768]{2,1,0:T(8,128)(2,1)}, bf16[3,256,768]{2,1,0:T(8,128)(2,1)}, f32[16,768]{1,0:T(8,128)}, f32[24,2304]{1,0:T(8,128)}, f32[24,768]{1,0:T...) custom-call(bf16[3,512,768]{2,1,0:T(8,128)(2,1)} %bitcast.36, s32[3,1,256]{2,1,0:T(1,128)} %keep.1, ...), custom_call_target="tpu_custom_call" | custom-call | flops 32614907904 | bytes 50000000 | tf_op jit(solution)/shard_map/layer/pallas_call | solution.py:1312
  252.2 5.9 %finish.1 = (bf16[3,256,768]{2,1,0:T(8,128)(2,1)}, f32[3,512,768]{2,1,0:T(8,128)}, f32[24,2304]{1,0:T(8,128)}, f32[24,768]{1,0:T(8,128)}, f32[24,3072]{1,0:T(8,1...) custom-call(s32[3,1,256]{2,1,0:T(1,128)} %keep.1, ...), custom_call_target="tpu_custom_call" | custom-call | tf_op jit(solution)/shard_map/finish/pallas_call | solution.py:1333
